TPU v7x, 32 devices: a whole 2x2x4 slice. The times are simulated.
32 devices in a mesh: parts: 2 (over y), off: 4 (over z), depth: 2 (over x), shot: 2 (over core).
Axes of the slice: x: 2, y: 2, z: 4, core: 2. Of those that a mesh axis runs over, the one named last changes fastest.
Arguments:
- image: bfloat16 [64, 32, 32, 256], P('off', None, 'depth'), may hold values from -4 to 4
- offset_of: int32 [64], P('off'), may hold values from 0 to 63, each once
- background: bfloat16 [4, 32, 32, 256], P(('parts', 'shot'), 'off', 'depth'), parts along dimension 0, may hold values from -6 to 6
- wave_now: float32 [4, 32, 32, 256], P(('parts', 'shot'), 'off', 'depth'), parts along dimension 0, may hold values from -6 to 6
- wave_prev: float32 [4, 32, 32, 256], P(('parts', 'shot'), 'off', 'depth'), parts along dimension 0, may hold values from -6 to 6
- courant: float32 [32, 32, 256], P('off', 'depth'), may hold values from 0.02 to 0.15
Outputs:
- wave_next: float32 [4, 32, 32, 256], P(('parts', 'shot'), 'off', 'depth'), parts along dimension 0
There are 2 independent parts, one for each index of `parts`. A program takes and returns all parts, laid end to end along the dimension named above; an argument that names none is the same for every part. Nothing has to cross between parts.
Inputs may be any that keep to these rules, and one draw needn't show every extreme that they name: Each value appears once; image column k holds offset offset_of[k] - 32 cells along x.
All inputs are finite; a program needn't handle non-finite values.
Results may differ from a plain program's by a relative error of at most 0.0003.
Values may be sent and summed in bfloat16 or wider, within the bound.
No kernel may reach another device: no remote copies, remote signals or barrier semaphores. Data moves between devices by JAX's collectives and lax.ppermute only.
A program may use at most 64 MiB of HBM per device.

v0:
```python
import jax
import jax.numpy as jnp
from jax import lax
from jax.sharding import PartitionSpec as P

H = 64


STENCIL = (-205.0 / 72.0, 8.0 / 5.0, -1.0 / 5.0, 8.0 / 315.0, -1.0 / 560.0)


def extended_2(cells, sides, width):
    for axis, dim in sides:
        count = lax.axis_size(axis)
        ends = count - 1
        head = lax.slice_in_dim(cells, 0, width, axis=dim)
        tail = lax.slice_in_dim(cells, cells.shape[dim] - width, cells.shape[dim], axis=dim)
        cells = jnp.concatenate(
            [
                lax.ppermute(tail, axis, [(i, (i + 1) % count) for i in range(ends)]),
                cells,
                lax.ppermute(head, axis, [((i + 1) % count, i) for i in range(ends)]),
            ],
            axis=dim,
        )
    return cells


def laplace(padded, rows_y, rows_z, cols_x):
    extended = jnp.pad(padded, ((0, 0), (0, 0), (4, 4)))
    centre = extended[4 : 4 + rows_y, 4 : 4 + rows_z, 4 : 4 + cols_x]
    running = 3.0 * STENCIL[0] * centre
    for radius in range(1, 5):
        beside_all = extended[4 + radius : 4 + radius + rows_y, 4 : 4 + rows_z, 4 : 4 + cols_x]
        beside_all = (
            beside_all + extended[4 - radius : 4 - radius + rows_y, 4 : 4 + rows_z, 4 : 4 + cols_x]
        )
        beside_all = (
            beside_all + extended[4 : 4 + rows_y, 4 + radius : 4 + radius + rows_z, 4 : 4 + cols_x]
        )
        beside_all = (
            beside_all + extended[4 : 4 + rows_y, 4 - radius : 4 - radius + rows_z, 4 : 4 + cols_x]
        )
        beside_all = (
            beside_all + extended[4 : 4 + rows_y, 4 : 4 + rows_z, 4 + radius : 4 + radius + cols_x]
        )
        beside_all = (
            beside_all + extended[4 : 4 + rows_y, 4 : 4 + rows_z, 4 - radius : 4 - radius + cols_x]
        )
        running = running + STENCIL[radius] * beside_all
    return running


def on_device(image, offset_of, background, wave_now, wave_prev, courant):
    slab_rows = wave_now.shape[1]
    depth_rows = wave_now.shape[2]
    width_x = wave_now.shape[3]
    local_cols = image.shape[0]
    half_span = H // 2
    gathered = lax.all_gather(background, "off", axis=1, tiled=True)
    extended_bg = jnp.pad(gathered[0], ((0, 0), (0, 0), (half_span, half_span)))
    first_index = jnp.asarray(jnp.int32(0), jnp.int32)

    def add_column(column, running):
        offset_cells = offset_of[column] - half_span
        whole_col = lax.dynamic_index_in_dim(image, column, 0, keepdims=False)
        starts = (first_index, jnp.zeros((), jnp.int32), half_span - offset_cells)
        shifted = lax.dynamic_slice(
            extended_bg, starts, (slab_rows * lax.axis_size("off"), depth_rows, width_x)
        )
        return running + whole_col.astype(jnp.float32) * shifted.astype(jnp.float32)

    own_source = lax.psum_scatter(
        lax.fori_loop(
            0,
            local_cols,
            add_column,
            jnp.zeros((slab_rows * lax.axis_size("off"), depth_rows, width_x), jnp.float32),
        ),
        "off",
        scatter_dimension=0,
        tiled=True,
    )
    padded = extended_2(wave_now[0], (("off", 0), ("depth", 1)), 4)
    bending = laplace(padded, slab_rows, depth_rows, width_x)
    stepped = 2.0 * wave_now[0] - wave_prev[0] + courant * (bending + own_source)
    return stepped[None]


def solution(mesh):
    return jax.shard_map(
        on_device,
        mesh=mesh,
        in_specs=(
            P("off", None, "depth", None),
            P("off"),
            P(("parts", "shot"), "off", "depth", None),
            P(("parts", "shot"), "off", "depth", None),
            P(("parts", "shot"), "off", "depth", None),
            P("off", "depth", None),
        ),
        out_specs=P(("parts", "shot"), "off", "depth", None),
        check_vma=False,
    )
```

profile of v0, /device:TPU:0, one launch (start us, length us, event | category | flops | bytes accessed | tf_op | source)
XLA Modules:
  0.0 105.4 jit_solution(5302099178217128605)
XLA Ops:
  6.5 15.8 %all_gather.3 = bf16[1,32,16,256]{3,2,0,1:T(8,128)(2,1)S(1)} all-gather(bf16[1,8,16,256]{3,2,0,1:T(8,128)(2,1)} %bitcast.29), channel_id=1, replica_groups=mesh['parts'=2,'off'=4,'depth'=2,'shot'=2] {'off'}, dimensions={1}, use_global_device_ids=true | all-gather | bytes 327680 | tf_op jit(solution)/shard_map/all_gather | solution.py:60
  22.6 50.0 %while.16 = (s32[]{:T(128)}, f32[32,16,256]{2,1,0:T(8,128)S(1)}, bf16[16,32,16,256]{3,2,1,0:T(8,128)(2,1)}, s32[16]{0:T(128)}, bf16[32,16,320]{2,1,0:T(8,128)(2,...) while((s32[]{:T(128)}, f32[32,16,256]{2,1,0:T(8,128)S(1)}, ...), condition=%wide.region_1.2_spmd.clone, body=%wide.region_0.1_spmd.clone.sunk | while | flops 655368 | bytes 1573061 | solution.py:74
  22.6 1.3 %dynamic_slice.41 = s32[1]{0:T(128)} dynamic-slice(s32[16]{0:T(128)} %get-tuple-element.227, s32[]{:T(128)S(6)} %copy.10), dynamic_slice_sizes={1} | dynamic-slice | bytes 12 | tf_op jit(solution)/shard_map/while/body/eval_jaxpr/dynamic_slice | solution.py:65
  25.8 1.3 %dynamic_slice.41 = s32[1]{0:T(128)} dynamic-slice(s32[16]{0:T(128)} %get-tuple-element.227, s32[]{:T(128)S(6)} %copy.10), dynamic_slice_sizes={1} | dynamic-slice | bytes 12 | tf_op jit(solution)/shard_map/while/body/eval_jaxpr/dynamic_slice | solution.py:65
  28.9 1.3 %dynamic_slice.41 = s32[1]{0:T(128)} dynamic-slice(s32[16]{0:T(128)} %get-tuple-element.227, s32[]{:T(128)S(6)} %copy.10), dynamic_slice_sizes={1} | dynamic-slice | bytes 12 | tf_op jit(solution)/shard_map/while/body/eval_jaxpr/dynamic_slice | solution.py:65
  32.1 1.3 %dynamic_slice.41 = s32[1]{0:T(128)} dynamic-slice(s32[16]{0:T(128)} %get-tuple-element.227, s32[]{:T(128)S(6)} %copy.10), dynamic_slice_sizes={1} | dynamic-slice | bytes 12 | tf_op jit(solution)/shard_map/while/body/eval_jaxpr/dynamic_slice | solution.py:65
  35.2 1.3 %dynamic_slice.41 = s32[1]{0:T(128)} dynamic-slice(s32[16]{0:T(128)} %get-tuple-element.227, s32[]{:T(128)S(6)} %copy.10), dynamic_slice_sizes={1} | dynamic-slice | bytes 12 | tf_op jit(solution)/shard_map/while/body/eval_jaxpr/dynamic_slice | solution.py:65
  38.3 1.3 %dynamic_slice.41 = s32[1]{0:T(128)} dynamic-slice(s32[16]{0:T(128)} %get-tuple-element.227, s32[]{:T(128)S(6)} %copy.10), dynamic_slice_sizes={1} | dynamic-slice | bytes 12 | tf_op jit(solution)/shard_map/while/body/eval_jaxpr/dynamic_slice | solution.py:65
  41.4 1.3 %dynamic_slice.41 = s32[1]{0:T(128)} dynamic-slice(s32[16]{0:T(128)} %get-tuple-element.227, s32[]{:T(128)S(6)} %copy.10), dynamic_slice_sizes={1} | dynamic-slice | bytes 12 | tf_op jit(solution)/shard_map/while/body/eval_jaxpr/dynamic_slice | solution.py:65
  44.5 1.3 %dynamic_slice.41 = s32[1]{0:T(128)} dynamic-slice(s32[16]{0:T(128)} %get-tuple-element.227, s32[]{:T(128)S(6)} %copy.10), dynamic_slice_sizes={1} | dynamic-slice | bytes 12 | tf_op jit(solution)/shard_map/while/body/eval_jaxpr/dynamic_slice | solution.py:65
  47.7 1.3 %dynamic_slice.41 = s32[1]{0:T(128)} dynamic-slice(s32[16]{0:T(128)} %get-tuple-element.227, s32[]{:T(128)S(6)} %copy.10), dynamic_slice_sizes={1} | dynamic-slice | bytes 12 | tf_op jit(solution)/shard_map/while/body/eval_jaxpr/dynamic_slice | solution.py:65
  50.8 1.3 %dynamic_slice.41 = s32[1]{0:T(128)} dynamic-slice(s32[16]{0:T(128)} %get-tuple-element.227, s32[]{:T(128)S(6)} %copy.10), dynamic_slice_sizes={1} | dynamic-slice | bytes 12 | tf_op jit(solution)/shard_map/while/body/eval_jaxpr/dynamic_slice | solution.py:65
  53.9 1.3 %dynamic_slice.41 = s32[1]{0:T(128)} dynamic-slice(s32[16]{0:T(128)} %get-tuple-element.227, s32[]{:T(128)S(6)} %copy.10), dynamic_slice_sizes={1} | dynamic-slice | bytes 12 | tf_op jit(solution)/shard_map/while/body/eval_jaxpr/dynamic_slice | solution.py:65
  63.2 1.3 %dynamic_slice.41 = s32[1]{0:T(128)} dynamic-slice(s32[16]{0:T(128)} %get-tuple-element.227, s32[]{:T(128)S(6)} %copy.10), dynamic_slice_sizes={1} | dynamic-slice | bytes 12 | tf_op jit(solution)/shard_map/while/body/eval_jaxpr/dynamic_slice | solution.py:65
  66.4 1.3 %dynamic_slice.41 = s32[1]{0:T(128)} dynamic-slice(s32[16]{0:T(128)} %get-tuple-element.227, s32[]{:T(128)S(6)} %copy.10), dynamic_slice_sizes={1} | dynamic-slice | bytes 12 | tf_op jit(solution)/shard_map/while/body/eval_jaxpr/dynamic_slice | solution.py:65
  69.5 1.3 %dynamic_slice.41 = s32[1]{0:T(128)} dynamic-slice(s32[16]{0:T(128)} %get-tuple-element.227, s32[]{:T(128)S(6)} %copy.10), dynamic_slice_sizes={1} | dynamic-slice | bytes 12 | tf_op jit(solution)/shard_map/while/body/eval_jaxpr/dynamic_slice | solution.py:65
  73.5 1.3 %collective-permute-start = (f32[4,16,256]{2,1,0:T(8,128)S(1)}, f32[4,16,256]{2,1,0:T(8,128)S(1)}, u32[]{:S(2)}, u32[]{:S(2)}) collective-permute-start(f32[4,16,256]{2,1,0:T(8,128)S(1)} %get-tuple-element.171), channel_id=1, source_target_pairs={{4,0},{8,4},{12,8},{5,1},{9,5},{13,9},{6,2},{10,6},{14,10},{7,3},{... | collective-permute-start | bytes 196616 | tf_op jit(solution)/shard_map/ppermute | solution.py:22
  74.8 4.5 %collective-permute-start.1 = (f32[4,16,256]{2,1,0:T(8,128)S(1)}, f32[4,16,256]{2,1,0:T(8,128)S(1)}, u32[]{:S(2)}, u32[]{:S(2)}) collective-permute-start(f32[4,16,256]{2,1,0:T(8,128)S(1)} %get-tuple-element.172), channel_id=1, source_target_pairs={{0,4},{4,8},{8,12},{1,5},{5,9},{9,13},{2,6},{6,10},{10,14},{3,7},{... | collective-permute-start | bytes 196616 | tf_op jit(solution)/shard_map/ppermute | solution.py:20
  79.6 2.0 %collective-permute-done.1 = f32[4,16,256]{2,1,0:T(8,128)S(1)} collective-permute-done((f32[4,16,256]{2,1,0:T(8,128)S(1)}, f32[4,16,256]{2,1,0:T(8,128)S(1)}, u32[]{:S(2)}, u32[]{:S(2)}) %collective-permute-start.1) | collective-permute-done | bytes 65568 | tf_op jit(solution)/shard_map/ppermute | solution.py:20
  81.6 3.0 %collective-permute-start.3 = (f32[16,4,256]{2,1,0:T(4,128)S(1)}, f32[16,4,256]{2,1,0:T(4,128)S(1)}, u32[]{:S(2)}, u32[]{:S(2)}) collective-permute-start(f32[16,4,256]{2,1,0:T(4,128)S(1)} %get-tuple-element.169), channel_id=1, source_target_pairs={{0,2},{1,3},{4,6},{5,7},{8,10},{9,11},{12,14},{13,15},{16,18},{17,... | collective-permute-start | bytes 196616 | tf_op jit(solution)/shard_map/ppermute | solution.py:20
  84.6 1.3 %collective-permute-start.2 = (f32[16,4,256]{2,1,0:T(4,128)S(1)}, f32[16,4,256]{2,1,0:T(4,128)S(1)}, u32[]{:S(2)}, u32[]{:S(2)}) collective-permute-start(f32[16,4,256]{2,1,0:T(4,128)S(1)} %get-tuple-element.170), channel_id=1, source_target_pairs={{2,0},{3,1},{6,4},{7,5},{10,8},{11,9},{14,12},{15,13},{18,16},{19,... | collective-permute-start | bytes 196616 | tf_op jit(solution)/shard_map/ppermute | solution.py:22
  86.5 4.3 %collective-permute-done.2 = f32[16,4,256]{2,1,0:T(4,128)S(1)} collective-permute-done((f32[16,4,256]{2,1,0:T(4,128)S(1)}, f32[16,4,256]{2,1,0:T(4,128)S(1)}, u32[]{:S(2)}, u32[]{:S(2)}) %collective-permute-start.2) | collective-permute-done | bytes 65568 | tf_op jit(solution)/shard_map/ppermute | solution.py:22
  91.2 5.5 %reduce-scatter.2.cloned.1.call-done = f32[8,16,256]{2,1,0:T(8,128)} async-done(((f32[32,16,256]{2,1,0:T(8,128)}), f32[8,16,256]{2,1,0:T(8,128)}) %reduce-scatter.2.cloned.1.call-update) | async-done | bytes 131088 | tf_op jit(solution)/shard_map/reduce_scatter | solution.py:73
  96.7 1.9 %fusion.14 = f32[1,8,16,256]{3,2,1,0:T(8,128)} fusion(f32[8,16,256]{2,1,0:T(8,128)S(1)} %copy-done.2, f32[8,16,256]{2,1,0:T(8,128)} %reduce-scatter.2.cloned.1.call-done, f32[8,16,256]{2,1,0:T(8,128)S(1)} %bitcast.27, f32[4,16,256]{2,1,0:T(8,128)S(1)} %collective-permute-done.1, f32[4,16,256]{2,1,0:T(8,128)S(1)} %collective-permute-done, ...), kind=kLoop, calls=%fused_computation.35 | loop fusion | flops 1376256 | bytes 2883584 | tf_op jit(solution)/shard_map/broadcast_in_dim | solution.py:87
  (36 shorter events, 23.9 us)
Async XLA Ops:
  6.5 90.1 %reduce-scatter.2.cloned.1.call-start = ((), (), s32[]{:S(2)}) async-start(), calls=%async_computation.1 | async-start | bytes 655360 | tf_op jit(solution)/shard_map/reduce_scatter | solution.py:73
  22.6 50.8 %copy-start.1 = (f32[1,8,16,256]{3,2,1,0:T(8,128)S(1)}, f32[1,8,16,256]{3,2,1,0:T(8,128)}, u32[]{:S(2)}) copy-start(f32[1,8,16,256]{3,2,1,0:T(8,128)} %param.11) | copy-start | bytes 393220
  22.6 74.1 %copy-start.2 = (f32[8,16,256]{2,1,0:T(8,128)S(1)}, f32[8,16,256]{2,1,0:T(8,128)}, u32[]{:S(2)}) copy-start(f32[8,16,256]{2,1,0:T(8,128)} %param.13) | copy-start | bytes 393220
  22.6 74.1 %copy-start.3 = (f32[1,8,16,256]{3,2,1,0:T(8,128)S(1)}, f32[1,8,16,256]{3,2,1,0:T(8,128)}, u32[]{:S(2)}) copy-start(f32[1,8,16,256]{3,2,1,0:T(8,128)} %param.12) | copy-start | bytes 393220
  72.6 0.8 copy-start
  73.5 6.2 %collective-permute-start = (f32[4,16,256]{2,1,0:T(8,128)S(1)}, f32[4,16,256]{2,1,0:T(8,128)S(1)}, u32[]{:S(2)}, u32[]{:S(2)}) collective-permute-start(f32[4,16,256]{2,1,0:T(8,128)S(1)} %get-tuple-element.171), channel_id=1, source_target_pairs={{4,0},{8,4},{12,8},{5,1},{9,5},{13,9},{6,2},{10,6},{14,10},{7,3},{... | collective-permute-start | bytes 196616 | tf_op jit(solution)/shard_map/ppermute | solution.py:22
  74.8 6.8 %collective-permute-start.1 = (f32[4,16,256]{2,1,0:T(8,128)S(1)}, f32[4,16,256]{2,1,0:T(8,128)S(1)}, u32[]{:S(2)}, u32[]{:S(2)}) collective-permute-start(f32[4,16,256]{2,1,0:T(8,128)S(1)} %get-tuple-element.172), channel_id=1, source_target_pairs={{0,4},{4,8},{8,12},{1,5},{5,9},{9,13},{2,6},{6,10},{10,14},{3,7},{... | collective-permute-start | bytes 196616 | tf_op jit(solution)/shard_map/ppermute | solution.py:20
  81.6 4.9 %collective-permute-start.3 = (f32[16,4,256]{2,1,0:T(4,128)S(1)}, f32[16,4,256]{2,1,0:T(4,128)S(1)}, u32[]{:S(2)}, u32[]{:S(2)}) collective-permute-start(f32[16,4,256]{2,1,0:T(4,128)S(1)} %get-tuple-element.169), channel_id=1, source_target_pairs={{0,2},{1,3},{4,6},{5,7},{8,10},{9,11},{12,14},{13,15},{16,18},{17,... | collective-permute-start | bytes 196616 | tf_op jit(solution)/shard_map/ppermute | solution.py:20
  84.6 6.2 %collective-permute-start.2 = (f32[16,4,256]{2,1,0:T(4,128)S(1)}, f32[16,4,256]{2,1,0:T(4,128)S(1)}, u32[]{:S(2)}, u32[]{:S(2)}) collective-permute-start(f32[16,4,256]{2,1,0:T(4,128)S(1)} %get-tuple-element.170), channel_id=1, source_target_pairs={{2,0},{3,1},{6,4},{7,5},{10,8},{11,9},{14,12},{15,13},{18,16},{19,... | collective-permute-start | bytes 196616 | tf_op jit(solution)/shard_map/ppermute | solution.py:22
Sparse Core Ops, SparseCore 0:
  73.5 23.0 reduce-scatter.1
where the time goes:
time: 106 us; the launch traced here: 105 us
  other arithmetic  21.3 us (20%)
  local copies, waits for them, and re-layouts  21.3 us (20%)
  blocking collectives  15.8 us (15%)
  between operations  13.5 us (13%)
  waiting for transfers between devices  12.6 us (12%)
  loops' own time  10.6 us (10%)
  starting transfers between devices  10.2 us (10%)
    dynamic_slice x16, local copies, waits for them, and re-layouts, add_column(): offset_cells = offset_of[column] - half_span  20.3 us
    add x16, other arithmetic, add_column(): return running + whole_col.astype(jnp.float32) * shifted.astype(jnp.float32)  19 us
    all_gather x1, blocking collectives, on_device(): gathered = lax.all_gather(background, 'off', axis=1, tiled=True)  15.8 us
    another operation x1, loops' own time, on_device(): lax.fori_loop(0, local_cols, add_column, jnp.zeros((slab_rows * lax.axis_...  10.6 us
    ppermute x2, starting transfers between devices, extended_2(): lax.ppermute(tail, axis, [(i, (i + 1) % count) for i in range(ends)])  7.58 us
    reduce_scatter x1, waiting for transfers between devices, on_device(): lax.psum_scatter(lax.fori_loop(0, local_cols, add_column, jnp.zeros((slab...  5.46 us
    ppermute x2, waiting for transfers between devices, extended_2(): lax.ppermute(head, axis, [((i + 1) % count, i) for i in range(ends)])  4.58 us
    ppermute x2, starting transfers between devices, extended_2(): lax.ppermute(head, axis, [((i + 1) % count, i) for i in range(ends)])  2.58 us
  transfers between devices with their start and end apart: 5, of which 5 were waited for; matrix products, arithmetic and copies ran while one was open for 0% of the time, Pallas kernels for 0%

commit v1 on v0

v1 whole, which is shorter than its diff:
```python
import functools

import jax
import jax.numpy as jnp
from jax import lax
from jax.experimental import pallas as pl
from jax.experimental.pallas import tpu as pltpu
from jax.sharding import PartitionSpec as P

STENCIL = (-205.0 / 72.0, 8.0 / 5.0, -1.0 / 5.0, 8.0 / 315.0, -1.0 / 560.0)
WIDTH = len(STENCIL) - 1

VMEM = pl.BlockSpec(memory_space=pltpu.VMEM)
SMEM = pl.BlockSpec(memory_space=pltpu.SMEM)
PARAMS = pltpu.CompilerParams(vmem_limit_bytes=32 * 2**20)


def source_kernel(half_span, slab_ref, offset_ref, image_ref, background_ref, out_ref):
    columns = image_ref.shape[0]
    rows, depth, width = background_ref.shape
    first_row = slab_ref[0] * rows
    lane = lax.broadcasted_iota(jnp.int32, (depth, width), 1)

    def add_column(column, running):
        cells = offset_ref[column] - half_span
        inside = (lane >= cells) & (lane < width + cells)
        amount = lax.rem(cells + width, width)
        result = []
        for row in range(rows):
            shifted = pltpu.roll(background_ref[row].astype(jnp.float32), amount, 1)
            shifted = jnp.where(inside, shifted, 0.0)
            result.append(
                running[row] + image_ref[column, first_row + row].astype(jnp.float32) * shifted
            )
        return tuple(result)

    zero = jnp.zeros((depth, width), jnp.float32)
    totals = lax.fori_loop(0, columns, add_column, (zero,) * rows, unroll=True)
    for row in range(rows):
        out_ref[row] = totals[row]


def source_of(image, offset_of, background, slab, half_span):
    return pl.pallas_call(
        functools.partial(source_kernel, half_span),
        out_shape=jax.ShapeDtypeStruct(background.shape, jnp.float32),
        in_specs=[SMEM, SMEM, VMEM, VMEM],
        out_specs=VMEM,
        compiler_params=PARAMS,
        cost_estimate=pl.CostEstimate(
            flops=2 * image.shape[0] * background.size,
            bytes_accessed=2 * image.shape[0] * background.size,
            transcendentals=0,
        ),
    )(slab.reshape(1), offset_of, image, background)


def step_kernel(
    ends_ref, now_ref, before_ref, after_ref, above_ref, below_ref, prev_ref, courant_ref, own_ref, out_ref, deep_ref
):
    rows, depth, width = now_ref.shape
    deep_ref[:, 2 * WIDTH : 2 * WIDTH + depth] = now_ref[...]
    deep_ref[:, WIDTH : 2 * WIDTH] = jnp.where(ends_ref[0] != 0, above_ref[...], 0.0)
    deep_ref[:, 2 * WIDTH + depth : 3 * WIDTH + depth] = jnp.where(
        ends_ref[1] != 0, below_ref[...], 0.0
    )
    lane = lax.broadcasted_iota(jnp.int32, (depth, width), 1)

    def layer(row):
        if row < 0:
            return before_ref[row + WIDTH]
        if row >= rows:
            return after_ref[row - rows]
        return now_ref[row]

    for row in range(rows):
        centre = now_ref[row]
        bending = 3.0 * STENCIL[0] * centre
        for radius in range(1, WIDTH + 1):
            beside = layer(row - radius) + layer(row + radius)
            beside = beside + deep_ref[row, 2 * WIDTH - radius : 2 * WIDTH - radius + depth]
            beside = beside + deep_ref[row, 2 * WIDTH + radius : 2 * WIDTH + radius + depth]
            left = jnp.where(lane >= radius, pltpu.roll(centre, radius, 1), 0.0)
            right = jnp.where(lane < width - radius, pltpu.roll(centre, width - radius, 1), 0.0)
            bending = bending + STENCIL[radius] * (beside + (left + right))
        out_ref[row] = 2.0 * centre - prev_ref[row] + courant_ref[row] * (bending + own_ref[row])


def neighbour_layers(cells, axis, dim):
    count = lax.axis_size(axis)
    here = lax.axis_index(axis)
    head = lax.slice_in_dim(cells, 0, WIDTH, axis=dim)
    tail = lax.slice_in_dim(cells, cells.shape[dim] - WIDTH, cells.shape[dim], axis=dim)
    if count == 2:
        other = lax.ppermute(jnp.where(here == 0, tail, head), axis, [(0, 1), (1, 0)])
        return other, other
    return (
        lax.ppermute(tail, axis, [(i, i + 1) for i in range(count - 1)]),
        lax.ppermute(head, axis, [(i + 1, i) for i in range(count - 1)]),
    )


def on_device(half_span, image, offset_of, background, wave_now, wave_prev, courant):
    groups = lax.axis_size("off")
    here = lax.axis_index("off").astype(jnp.int32)
    depth_at = lax.axis_index("depth")
    own_slab, now, prev = background[0], wave_now[0], wave_prev[0]

    slabs = [
        lax.ppermute(own_slab, "off", [(i, (i + step) % groups) for i in range(groups)])
        for step in range(1, groups)
    ]
    before, after = neighbour_layers(now, "off", 0)
    above, below = neighbour_layers(now, "depth", 1)
    ends = jnp.stack([depth_at != 0, depth_at != lax.axis_size("depth") - 1]).astype(jnp.int32)

    own = source_of(image, offset_of, own_slab, here, half_span)
    rows, depth, width = now.shape
    base = pl.pallas_call(
        step_kernel,
        out_shape=jax.ShapeDtypeStruct(now.shape, jnp.float32),
        in_specs=[SMEM] + [VMEM] * 8,
        out_specs=VMEM,
        scratch_shapes=[pltpu.VMEM((rows, depth + 4 * WIDTH, width), jnp.float32)],
        compiler_params=PARAMS,
        cost_estimate=pl.CostEstimate(
            flops=40 * now.size, bytes_accessed=24 * now.size, transcendentals=0
        ),
    )(ends, now, before, after, above, below, prev, courant, own)

    returned = []
    for step in range(1, groups):
        slab = lax.rem(here - step + groups, groups)
        part = source_of(image, offset_of, slabs[step - 1], slab, half_span)
        returned.append(
            lax.ppermute(part, "off", [(i, (i - step) % groups) for i in range(groups)])
        )
    stepped = base + courant * functools.reduce(jnp.add, returned)
    return stepped[None]


def solution(mesh):
    def whole(image, offset_of, background, wave_now, wave_prev, courant):
        return jax.shard_map(
            functools.partial(on_device, offset_of.shape[0] // 2),
            mesh=mesh,
            in_specs=(
                P("off", None, "depth", None),
                P("off"),
                P(("parts", "shot"), "off", "depth", None),
                P(("parts", "shot"), "off", "depth", None),
                P(("parts", "shot"), "off", "depth", None),
                P("off", "depth", None),
            ),
            out_specs=P(("parts", "shot"), "off", "depth", None),
            check_vma=False,
        )(image, offset_of, background, wave_now, wave_prev, courant)

    return whole
```

time: 106 us -> 34.4 us (0.32)
  other arithmetic: 21.3 us -> 1.67 us
  local copies, waits for them, and re-layouts: 21.3 us -> 5.05 us
  blocking collectives: 15.8 us -> 0 us
  between operations: 13.5 us -> 0.14 us
  loops' own time: 10.6 us -> 0 us
  waiting for transfers between devices: 12.6 us -> 4.8 us
  starting transfers between devices: 10.2 us -> 17.1 us
  Pallas kernels: 0 us -> 5.41 us
    dynamic_slice x16 -> x0, local copies, waits for them, and re-layouts: 20.3 us -> none  [add_column(): offset_cells = offset_of[column] - half_span]
    add x16 -> x0, other arithmetic: 19 us -> none  [add_column(): return running + whole_col.astype(jnp.float32) * shifted.astype(jnp.float32)]
    all_gather x1 -> x0, blocking collectives: 15.8 us -> none  [on_device(): gathered = lax.all_gather(background, 'off', axis=1, tiled=True)]
    another operation x1 -> x0, loops' own time: 10.6 us -> none  [on_device(): lax.fori_loop(0, local_cols, add_column, jnp.zeros((slab_rows * lax.axis_...]
    ppermute x4 -> x9, starting transfers between devices: 10.2 us -> 17.1 us  [the longest x3 6.06 us: on_device(): lax.ppermute(own_slab, 'off', [(i, (i + step) % groups) for i in range(gr...]
    reduce_scatter x1 -> x0, waiting for transfers between devices: 5.46 us -> none  [on_device(): lax.psum_scatter(lax.fori_loop(0, local_cols, add_column, jnp.zeros((slab...]
    pallas_call x0 -> x5, Pallas kernels: none -> 5.41 us  [the longest x4 4.5 us: source_of(): pl.pallas_call(functools.partial(source_kernel, half_span), out_shape=jax...]
    unnamed x8 -> x16, local copies, waits for them, and re-layouts: 0.82 us -> 5.04 us
  transfers between devices with their start and end apart: 5 -> 9, of which waited for: 5 -> 1; matrix products, arithmetic and copies ran while one was open for 0% -> 3% of each run, Pallas kernels for 0% -> 16%
where the time goes in v1:
time: 34.4 us; the launch traced here: 34.2 us
  starting transfers between devices  17.1 us (50%)
  Pallas kernels  5.41 us (16%)
  local copies, waits for them, and re-layouts  5.05 us (15%)
  waiting for transfers between devices  4.8 us (14%)
  other arithmetic  1.67 us (5%)
    ppermute x3, starting transfers between devices, on_device(): lax.ppermute(own_slab, 'off', [(i, (i + step) % groups) for i in range(gr...  6.06 us
    ppermute x3, starting transfers between devices, on_device(): lax.ppermute(part, 'off', [(i, (i - step) % groups) for i in range(groups)])  5.05 us
    unnamed x16, local copies, waits for them, and re-layouts  5.04 us
    ppermute x1, waiting for transfers between devices, neighbour_layers(): lax.ppermute(head, axis, [(i + 1, i) for i in range(count - 1)])  4.78 us
    pallas_call x4, Pallas kernels, source_of(): pl.pallas_call(functools.partial(source_kernel, half_span), out_shape=jax...  4.5 us
    ppermute x1, starting transfers between devices, neighbour_layers(): lax.ppermute(tail, axis, [(i, i + 1) for i in range(count - 1)])  3.14 us
    ppermute x1, starting transfers between devices, neighbour_layers(): lax.ppermute(jnp.where(here == 0, tail, head), axis, [(0, 1), (1, 0)])  1.56 us
    ppermute x1, starting transfers between devices, neighbour_layers(): lax.ppermute(head, axis, [(i + 1, i) for i in range(count - 1)])  1.29 us
  transfers between devices with their start and end apart: 9, of which 1 were waited for; matrix products, arithmetic and copies ran while one was open for 3% of the time, Pallas kernels for 16%

profile of v1, /device:TPU:0, one launch (start us, length us, event | category | flops | bytes accessed | tf_op | source)
XLA Modules:
  0.0 34.2 jit_solution(3185882801189728118)
XLA Ops:
  0.0 5.0 %collective-permute-start.7 = (bf16[8,16,256]{2,1,0:T(8,128)(2,1)}, bf16[8,16,256]{2,1,0:T(8,128)(2,1)S(1)}, u32[]{:S(2)}, u32[]{:S(2)}) collective-permute-start(bf16[8,16,256]{2,1,0:T(8,128)(2,1)} %bitcast.18), channel_id=1, source_target_pairs={{0,12},{4,0},{8,4},{12,8},{1,13},{5,1},{9,5},{13,9},{2,14},{6,2},{... | collective-permute-start | bytes 196616 | tf_op jit(solution)/shard_map/ppermute | solution.py:110
  5.1 1.0 %collective-permute-start.5 = (bf16[8,16,256]{2,1,0:T(8,128)(2,1)}, bf16[8,16,256]{2,1,0:T(8,128)(2,1)S(1)}, u32[]{:S(2)}, u32[]{:S(2)}) collective-permute-start(bf16[8,16,256]{2,1,0:T(8,128)(2,1)} %bitcast.20), channel_id=1, source_target_pairs={{0,8},{4,12},{8,0},{12,4},{1,9},{5,13},{9,1},{13,5},{2,10},{6,14},... | collective-permute-start | bytes 196616 | tf_op jit(solution)/shard_map/ppermute | solution.py:110
  6.1 0.9 %slice_select_fusion = f32[8,4,256]{2,1,0:T(4,128)S(1)} fusion(f32[8,16,256]{2,1,0:T(8,128)} %bitcast.15, pred[]{:T(512)S(6)} %eq.3), kind=kLoop, calls=%fused_computation.3 | loop fusion | flops 8192 | bytes 98305 | tf_op jit(solution)/shard_map/jit(_where)/select_n | solution.py:95
  6.9 1.6 %collective-permute-start.2 = (f32[8,4,256]{2,1,0:T(4,128)S(1)}, f32[8,4,256]{2,1,0:T(4,128)S(1)}, u32[]{:S(2)}, u32[]{:S(2)}) collective-permute-start(f32[8,4,256]{2,1,0:T(4,128)S(1)} %slice_select_fusion), channel_id=1, source_target_pairs={{0,2},{2,0},{1,3},{3,1},{4,6},{6,4},{5,7},{7,5},{8,10},{10,8},{9,1... | collective-permute-start | bytes 98312 | tf_op jit(solution)/shard_map/ppermute | solution.py:95
  8.5 2.2 %copy-done = bf16[16,32,16,256]{3,2,1,0:T(8,128)(2,1)S(1)} copy-done((bf16[16,32,16,256]{3,2,1,0:T(8,128)(2,1)S(1)}, bf16[16,32,16,256]{3,2,1,0:T(8,128)(2,1)}, u32[]{:S(2)}) %copy-start) | copy-done | bytes 4194328
  10.7 0.7 %copy-done.6 = s32[16]{0:T(128)S(1)} copy-done((s32[16]{0:T(128)S(1)}, s32[16]{0:T(128)}, u32[]{:S(2)}) %copy-start.6) | copy-done | bytes 88
  11.4 1.1 %shard_map.68 = f32[8,16,256]{2,1,0:T(8,128)S(1)} custom-call(s32[1]{0:T(128)} %bitcast.10.slab_ref, s32[16]{0:T(128)S(1)} %copy-done.6, bf16[16,32,16,256]{3,2,1,0:T(8,128)(2,1)S(1)} %copy-done, bf16[8,16,256]{2,1,0:T(8,128)(2,1)S(1)} %collective-permute-done.7.background_ref), custom_call_target="tpu_custom_call" | custom-call | flops 1048576 | bytes 1048576 | tf_op jit(solution)/shard_map/pallas_call | solution.py:44
  12.5 3.4 %collective-permute-start.8 = (f32[8,16,256]{2,1,0:T(8,128)S(1)}, f32[8,16,256]{2,1,0:T(8,128)S(1)}, u32[]{:S(2)}, u32[]{:S(2)}) collective-permute-start(f32[8,16,256]{2,1,0:T(8,128)S(1)} %shard_map.68), channel_id=1, source_target_pairs={{0,4},{4,8},{8,12},{12,0},{1,5},{5,9},{9,13},{13,1},{2,6},{6,10},{... | collective-permute-start | bytes 393224 | tf_op jit(solution)/shard_map/ppermute | solution.py:136
  15.9 0.0 collective-permute-done.3.background_ref
  15.9 1.1 %shard_map.66 = f32[8,16,256]{2,1,0:T(8,128)S(1)} custom-call(s32[1]{0:T(128)} %bitcast.8.slab_ref, s32[16]{0:T(128)S(1)} %copy-done.6, bf16[16,32,16,256]{3,2,1,0:T(8,128)(2,1)S(1)} %copy-done, bf16[8,16,256]{2,1,0:T(8,128)(2,1)S(1)} %collective-permute-done.3.background_ref), custom_call_target="tpu_custom_call" | custom-call | flops 1048576 | bytes 1048576 | tf_op jit(solution)/shard_map/pallas_call | solution.py:44
  17.1 0.5 %collective-permute-start.4 = (f32[8,16,256]{2,1,0:T(8,128)S(1)}, f32[8,16,256]{2,1,0:T(8,128)S(1)}, u32[]{:S(2)}, u32[]{:S(2)}) collective-permute-start(f32[8,16,256]{2,1,0:T(8,128)S(1)} %shard_map.66), channel_id=1, source_target_pairs={{0,12},{4,0},{8,4},{12,8},{1,13},{5,1},{9,5},{13,9},{2,14},{6,2},{... | collective-permute-start | bytes 393224 | tf_op jit(solution)/shard_map/ppermute | solution.py:136
  17.6 0.0 collective-permute-done.5.background_ref
  17.6 1.1 %shard_map.67 = f32[8,16,256]{2,1,0:T(8,128)S(1)} custom-call(s32[1]{0:T(128)} %bitcast.9.slab_ref, s32[16]{0:T(128)S(1)} %copy-done.6, bf16[16,32,16,256]{3,2,1,0:T(8,128)(2,1)S(1)} %copy-done, bf16[8,16,256]{2,1,0:T(8,128)(2,1)S(1)} %collective-permute-done.5.background_ref), custom_call_target="tpu_custom_call" | custom-call | flops 1048576 | bytes 1048576 | tf_op jit(solution)/shard_map/pallas_call | solution.py:44
  18.7 1.1 %collective-permute-start.6 = (f32[8,16,256]{2,1,0:T(8,128)S(1)}, f32[8,16,256]{2,1,0:T(8,128)S(1)}, u32[]{:S(2)}, u32[]{:S(2)}) collective-permute-start(f32[8,16,256]{2,1,0:T(8,128)S(1)} %shard_map.67), channel_id=1, source_target_pairs={{0,8},{4,12},{8,0},{12,4},{1,9},{5,13},{9,1},{13,5},{2,10},{6,14},... | collective-permute-start | bytes 393224 | tf_op jit(solution)/shard_map/ppermute | solution.py:136
  19.8 3.1 %collective-permute-start = (f32[4,16,256]{2,1,0:T(8,128)S(1)}, f32[4,16,256]{2,1,0:T(8,128)S(1)}, u32[]{:S(2)}, u32[]{:S(2)}) collective-permute-start(f32[4,16,256]{2,1,0:T(8,128)S(1)} %get-tuple-element.6), channel_id=1, source_target_pairs={{0,4},{4,8},{8,12},{1,5},{5,9},{9,13},{2,6},{6,10},{10,14},{3,7},{... | collective-permute-start | bytes 196616 | tf_op jit(solution)/shard_map/ppermute | solution.py:98
  23.0 0.0 copy-start.1
  23.0 2.2 %copy-done.1 = bf16[16,32,16,256]{3,2,1,0:T(8,128)(2,1)S(1)} copy-done((bf16[16,32,16,256]{3,2,1,0:T(8,128)(2,1)S(1)}, bf16[16,32,16,256]{3,2,1,0:T(8,128)(2,1)}, u32[]{:S(2)}) %copy-start.1) | copy-done | bytes 4194328
  25.2 1.1 %shard_map.64.own_ref = f32[8,16,256]{2,1,0:T(8,128)S(1)} custom-call(s32[1]{0:T(128)} %bitcast.6.slab_ref, s32[16]{0:T(128)S(1)} %copy-done.7, bf16[16,32,16,256]{3,2,1,0:T(8,128)(2,1)S(1)} %copy-done.1, bf16[8,16,256]{2,1,0:T(8,128)(2,1)S(1)} %bitcast.21), custom_call_target="tpu_custom_call" | custom-call | flops 1048576 | bytes 1048576 | tf_op jit(solution)/shard_map/pallas_call | solution.py:44
  26.3 1.3 %collective-permute-start.1 = (f32[4,16,256]{2,1,0:T(8,128)S(1)}, f32[4,16,256]{2,1,0:T(8,128)S(1)}, u32[]{:S(2)}, u32[]{:S(2)}) collective-permute-start(f32[4,16,256]{2,1,0:T(8,128)S(1)} %get-tuple-element.5), channel_id=1, source_target_pairs={{4,0},{8,4},{12,8},{5,1},{9,5},{13,9},{6,2},{10,6},{14,10},{7,3},{... | collective-permute-start | bytes 196616 | tf_op jit(solution)/shard_map/ppermute | solution.py:99
  27.6 0.1 add_convert_fusion.ends_ref
  27.7 4.8 %collective-permute-done.1.after_ref = f32[4,16,256]{2,1,0:T(8,128)S(1)} collective-permute-done((f32[4,16,256]{2,1,0:T(8,128)S(1)}, f32[4,16,256]{2,1,0:T(8,128)S(1)}, u32[]{:S(2)}, u32[]{:S(2)}) %collective-permute-start.1) | collective-permute-done | bytes 65568 | tf_op jit(solution)/shard_map/ppermute | solution.py:99
  32.5 0.9 %shard_map.65 = f32[8,16,256]{2,1,0:T(8,128)S(1)} custom-call(s32[2]{0:T(128)S(1)} %add_convert_fusion.ends_ref, f32[8,16,256]{2,1,0:T(8,128)S(1)} %bitcast.16, f32[4,16,256]{2,1,0:T(8,128)S(1)} %collective-permute-done.before_ref, f32[4,16,256]{2,1,0:T(8,128)S(1)} %collective-permute-done.1.after_ref, ...), custom_call_target="tpu_custom_call" | custom-call | flops 1310720 | bytes 786432 | tf_op jit(solution)/shard_map/pallas_call | solution.py:119
  33.4 0.0 collective-permute-done.4
  33.5 0.7 %add_bitcast_fusion = f32[1,8,16,256]{3,2,1,0:T(8,128)} fusion(f32[8,16,256]{2,1,0:T(8,128)S(1)} %shard_map.65, f32[8,16,256]{2,1,0:T(8,128)S(1)} %copy-done.3, f32[8,16,256]{2,1,0:T(8,128)S(1)} %collective-permute-done.8, f32[8,16,256]{2,1,0:T(8,128)S(1)} %collective-permute-done.4, f32[8,16,256]{2,1,0:T(8,128)S(1)} %collective-permute-done.6), kind=kLoop, calls=%fused_computation | loop fusion | flops 131072 | bytes 786432 | tf_op jit(solution)/shard_map/broadcast_in_dim | solution.py:139
  (19 shorter events, 0.0 us)
Async XLA Ops:
  0.0 8.5 %collective-permute-start.7 = (bf16[8,16,256]{2,1,0:T(8,128)(2,1)}, bf16[8,16,256]{2,1,0:T(8,128)(2,1)S(1)}, u32[]{:S(2)}, u32[]{:S(2)}) collective-permute-start(bf16[8,16,256]{2,1,0:T(8,128)(2,1)} %bitcast.18), channel_id=1, source_target_pairs={{0,12},{4,0},{8,4},{12,8},{1,13},{5,1},{9,5},{13,9},{2,14},{6,2},{... | collective-permute-start | bytes 196616 | tf_op jit(solution)/shard_map/ppermute | solution.py:110
  5.0 10.9 %collective-permute-start.3 = (bf16[8,16,256]{2,1,0:T(8,128)(2,1)}, bf16[8,16,256]{2,1,0:T(8,128)(2,1)S(1)}, u32[]{:S(2)}, u32[]{:S(2)}) collective-permute-start(bf16[8,16,256]{2,1,0:T(8,128)(2,1)} %bitcast.19), channel_id=1, source_target_pairs={{0,4},{4,8},{8,12},{12,0},{1,5},{5,9},{9,13},{13,1},{2,6},{6,10},{... | collective-permute-start | bytes 196616 | tf_op jit(solution)/shard_map/ppermute | solution.py:110
  5.1 12.5 %collective-permute-start.5 = (bf16[8,16,256]{2,1,0:T(8,128)(2,1)}, bf16[8,16,256]{2,1,0:T(8,128)(2,1)S(1)}, u32[]{:S(2)}, u32[]{:S(2)}) collective-permute-start(bf16[8,16,256]{2,1,0:T(8,128)(2,1)} %bitcast.20), channel_id=1, source_target_pairs={{0,8},{4,12},{8,0},{12,4},{1,9},{5,13},{9,1},{13,5},{2,10},{6,14},... | collective-permute-start | bytes 196616 | tf_op jit(solution)/shard_map/ppermute | solution.py:110
  6.9 19.4 %collective-permute-start.2 = (f32[8,4,256]{2,1,0:T(4,128)S(1)}, f32[8,4,256]{2,1,0:T(4,128)S(1)}, u32[]{:S(2)}, u32[]{:S(2)}) collective-permute-start(f32[8,4,256]{2,1,0:T(4,128)S(1)} %slice_select_fusion), channel_id=1, source_target_pairs={{0,2},{2,0},{1,3},{3,1},{4,6},{6,4},{5,7},{7,5},{8,10},{10,8},{9,1... | collective-permute-start | bytes 98312 | tf_op jit(solution)/shard_map/ppermute | solution.py:95
  8.5 2.2 %copy-start = (bf16[16,32,16,256]{3,2,1,0:T(8,128)(2,1)S(1)}, bf16[16,32,16,256]{3,2,1,0:T(8,128)(2,1)}, u32[]{:S(2)}) copy-start(bf16[16,32,16,256]{3,2,1,0:T(8,128)(2,1)} %image_ref.7) | copy-start | bytes 12582916
  10.7 0.7 %copy-start.6 = (s32[16]{0:T(128)S(1)}, s32[16]{0:T(128)}, u32[]{:S(2)}) copy-start(s32[16]{0:T(128)} %offset_ref.7) | copy-start | bytes 196
  12.5 21.0 %collective-permute-start.8 = (f32[8,16,256]{2,1,0:T(8,128)S(1)}, f32[8,16,256]{2,1,0:T(8,128)S(1)}, u32[]{:S(2)}, u32[]{:S(2)}) collective-permute-start(f32[8,16,256]{2,1,0:T(8,128)S(1)} %shard_map.68), channel_id=1, source_target_pairs={{0,4},{4,8},{8,12},{12,0},{1,5},{5,9},{9,13},{13,1},{2,6},{6,10},{... | collective-permute-start | bytes 393224 | tf_op jit(solution)/shard_map/ppermute | solution.py:136
  15.9 3.9 %copy-start.2 = (f32[1,8,16,256]{3,2,1,0:T(8,128)S(1)}, f32[1,8,16,256]{3,2,1,0:T(8,128)}, u32[]{:S(2)}) copy-start(f32[1,8,16,256]{3,2,1,0:T(8,128)} %param.9) | copy-start | bytes 393220
  15.9 7.1 %copy-start.5 = (bf16[1,8,16,256]{3,2,1,0:T(8,128)(2,1)S(1)}, bf16[1,8,16,256]{3,2,1,0:T(8,128)(2,1)}, u32[]{:S(2)}) copy-start(bf16[1,8,16,256]{3,2,1,0:T(8,128)(2,1)} %param.8) | copy-start | bytes 196612
  15.9 7.1 %copy-start.7 = (s32[16]{0:T(128)S(1)}, s32[16]{0:T(128)}, u32[]{:S(2)}) copy-start(s32[16]{0:T(128)} %offset_ref.7) | copy-start | bytes 196
  17.1 16.4 %collective-permute-start.4 = (f32[8,16,256]{2,1,0:T(8,128)S(1)}, f32[8,16,256]{2,1,0:T(8,128)S(1)}, u32[]{:S(2)}, u32[]{:S(2)}) collective-permute-start(f32[8,16,256]{2,1,0:T(8,128)S(1)} %shard_map.66), channel_id=1, source_target_pairs={{0,12},{4,0},{8,4},{12,8},{1,13},{5,1},{9,5},{13,9},{2,14},{6,2},{... | collective-permute-start | bytes 393224 | tf_op jit(solution)/shard_map/ppermute | solution.py:136
  17.6 14.9 %copy-start.3 = (f32[8,16,256]{2,1,0:T(8,128)S(1)}, f32[8,16,256]{2,1,0:T(8,128)}, u32[]{:S(2)}) copy-start(f32[8,16,256]{2,1,0:T(8,128)} %courant_ref.1) | copy-start | bytes 393220
  17.6 14.9 %copy-start.4 = (f32[1,8,16,256]{3,2,1,0:T(8,128)S(1)}, f32[1,8,16,256]{3,2,1,0:T(8,128)}, u32[]{:S(2)}) copy-start(f32[1,8,16,256]{3,2,1,0:T(8,128)} %param.10) | copy-start | bytes 393220
  18.7 14.8 %collective-permute-start.6 = (f32[8,16,256]{2,1,0:T(8,128)S(1)}, f32[8,16,256]{2,1,0:T(8,128)S(1)}, u32[]{:S(2)}, u32[]{:S(2)}) collective-permute-start(f32[8,16,256]{2,1,0:T(8,128)S(1)} %shard_map.67), channel_id=1, source_target_pairs={{0,8},{4,12},{8,0},{12,4},{1,9},{5,13},{9,1},{13,5},{2,10},{6,14},... | collective-permute-start | bytes 393224 | tf_op jit(solution)/shard_map/ppermute | solution.py:136
  19.8 7.9 %collective-permute-start = (f32[4,16,256]{2,1,0:T(8,128)S(1)}, f32[4,16,256]{2,1,0:T(8,128)S(1)}, u32[]{:S(2)}, u32[]{:S(2)}) collective-permute-start(f32[4,16,256]{2,1,0:T(8,128)S(1)} %get-tuple-element.6), channel_id=1, source_target_pairs={{0,4},{4,8},{8,12},{1,5},{5,9},{9,13},{2,6},{6,10},{10,14},{3,7},{... | collective-permute-start | bytes 196616 | tf_op jit(solution)/shard_map/ppermute | solution.py:98
  23.0 2.2 %copy-start.1 = (bf16[16,32,16,256]{3,2,1,0:T(8,128)(2,1)S(1)}, bf16[16,32,16,256]{3,2,1,0:T(8,128)(2,1)}, u32[]{:S(2)}) copy-start(bf16[16,32,16,256]{3,2,1,0:T(8,128)(2,1)} %image_ref.7) | copy-start | bytes 12582916
  26.3 6.2 %collective-permute-start.1 = (f32[4,16,256]{2,1,0:T(8,128)S(1)}, f32[4,16,256]{2,1,0:T(8,128)S(1)}, u32[]{:S(2)}, u32[]{:S(2)}) collective-permute-start(f32[4,16,256]{2,1,0:T(8,128)S(1)} %get-tuple-element.5), channel_id=1, source_target_pairs={{4,0},{8,4},{12,8},{5,1},{9,5},{13,9},{6,2},{10,6},{14,10},{7,3},{... | collective-permute-start | bytes 196616 | tf_op jit(solution)/shard_map/ppermute | solution.py:99

commit v2 on v1

v2 whole, which is shorter than its diff:
```python
import functools

import jax
import jax.numpy as jnp
from jax import lax
from jax.experimental import pallas as pl
from jax.experimental.pallas import tpu as pltpu
from jax.sharding import PartitionSpec as P

STENCIL = (-205.0 / 72.0, 8.0 / 5.0, -1.0 / 5.0, 8.0 / 315.0, -1.0 / 560.0)
WIDTH = len(STENCIL) - 1
LANES = 128
MIB = 2**20

VMEM = pl.BlockSpec(memory_space=pltpu.VMEM)
SMEM = pl.BlockSpec(memory_space=pltpu.SMEM)
ANY = pl.BlockSpec(memory_space=pl.ANY)
COST = pl.CostEstimate(flops=1000, bytes_accessed=1000, transcendentals=0)


def add_column(half_span, offset_ref, image_ref, background_ref, first_row, column, running):
    rows, depth, width = background_ref.shape
    cells = offset_ref[column] - half_span
    back = cells < 0
    turn = jnp.where(back, cells + LANES, cells)
    wrapped = lax.broadcasted_iota(jnp.int32, (depth, LANES), 1) < turn
    result = []
    for row in range(rows):
        turned = [
            pltpu.roll(background_ref[row, :, start : start + LANES], turn, 1)
            for start in range(0, width, LANES)
        ]
        zero = jnp.zeros_like(turned[0])
        ahead = [zero] + turned
        behind = turned + [zero]
        chosen = [jnp.where(back, b, a) for a, b in zip(ahead, behind)]
        shifted = [jnp.where(wrapped, a, b) for a, b in zip(chosen[:-1], chosen[1:])]
        factor = image_ref[column, first_row + row].astype(jnp.float32)
        result.append(running[row] + factor * jnp.concatenate(shifted, 1).astype(jnp.float32))
    return tuple(result)


def first_kernel(half_span, offset_ref, image_ref, background_ref, now_ref, out_ref, held_ref, layers_ref, cells_ref, slab_ref, arrived, sem):
    columns = image_ref.shape[0]
    rows, depth, width = slab_ref.shape
    before = (
        pltpu.make_async_copy(offset_ref, cells_ref, sem.at[0]),
        pltpu.make_async_copy(background_ref, slab_ref, sem.at[1]),
    )
    wave = pltpu.make_async_copy(now_ref, layers_ref, sem.at[2])
    copies = [
        pltpu.make_async_copy(image_ref.at[column], held_ref.at[column], arrived.at[column])
        for column in range(columns)
    ]
    for copy in before + (wave,) + tuple(copies):
        copy.start()
    for copy in before:
        copy.wait()
    first_row = lax.axis_index("off") * rows
    add = functools.partial(add_column, half_span, cells_ref, held_ref, slab_ref, first_row)
    totals = (jnp.zeros((depth, width), jnp.float32),) * rows
    for column, copy in enumerate(copies):
        copy.wait()
        totals = add(column, totals)
    for row in range(rows):
        out_ref[row] = totals[row]
    wave.wait()


def first_source(image, offset_of, background, now, half_span):
    return pl.pallas_call(
        functools.partial(first_kernel, half_span),
        out_shape=(
            pltpu.VMEM(background.shape, jnp.float32),
            pltpu.VMEM(image.shape, image.dtype),
            pltpu.VMEM(now.shape, now.dtype),
            pltpu.SMEM(offset_of.shape, offset_of.dtype),
        ),
        in_specs=[ANY] * 4,
        out_specs=(VMEM, VMEM, VMEM, SMEM),
        scratch_shapes=[
            pltpu.VMEM(background.shape, background.dtype),
            pltpu.SemaphoreType.DMA((image.shape[0],)),
            pltpu.SemaphoreType.DMA((3,)),
        ],
        compiler_params=pltpu.CompilerParams(vmem_limit_bytes=32 * MIB),
        cost_estimate=COST,
    )(*[pltpu.with_memory_space_constraint(x, pltpu.HBM) for x in (offset_of, image, background, now)])


def source_kernel(half_span, step, groups, offset_ref, image_ref, background_ref, now_ref, earlier_ref, out_ref):
    del earlier_ref
    rows, depth, width = background_ref.shape
    here = lax.axis_index("off")
    slab = lax.rem(here - step + groups, groups)
    add = functools.partial(
        add_column, half_span, offset_ref, image_ref, background_ref, slab * rows
    )
    totals = (jnp.zeros((depth, width), jnp.float32),) * rows
    for column in range(image_ref.shape[0]):
        totals = add(column, totals)
    for row in range(rows):
        out_ref[row] = totals[row]
    at = rows
    if step == 1:
        for layer in range(WIDTH):
            out_ref[at + layer] = jnp.where(here != 0, now_ref[layer], 0.0)
        at += WIDTH
    if step == groups - 1:
        for layer in range(WIDTH):
            out_ref[at + layer] = jnp.where(
                here != groups - 1, now_ref[rows - WIDTH + layer], 0.0
            )


def source_of(image, offset_of, background, now, earlier, step, groups, half_span):
    rows, depth, width = background.shape
    extra = WIDTH * ((step == 1) + (step == groups - 1))
    return pl.pallas_call(
        functools.partial(source_kernel, half_span, step, groups),
        out_shape=pltpu.VMEM((rows + extra, depth, width), jnp.float32),
        in_specs=[SMEM, VMEM, VMEM, VMEM, ANY],
        out_specs=VMEM,
        compiler_params=pltpu.CompilerParams(vmem_limit_bytes=32 * MIB),
        cost_estimate=COST,
    )(offset_of, image, background, now, earlier)


def step_kernel(now_ref, above_ref, below_ref, prev_ref, courant_ref, own_ref, out_ref, deep_ref):
    rows, depth, width = now_ref.shape
    at = lax.axis_index("depth")
    deep_ref[:, 2 * WIDTH : 2 * WIDTH + depth] = now_ref[...]
    deep_ref[:, WIDTH : 2 * WIDTH] = jnp.where(
        at != 0, above_ref[:, depth - WIDTH :], 0.0
    )
    deep_ref[:, 2 * WIDTH + depth : 3 * WIDTH + depth] = jnp.where(
        at != lax.axis_size("depth") - 1, below_ref[:, :WIDTH], 0.0
    )
    lane = lax.broadcasted_iota(jnp.int32, (depth, width), 1)
    for row in range(rows):
        centre = now_ref[row]
        bending = 3.0 * STENCIL[0] * centre
        for radius in range(1, WIDTH + 1):
            beside = deep_ref[row, 2 * WIDTH - radius : 2 * WIDTH - radius + depth]
            beside = beside + deep_ref[row, 2 * WIDTH + radius : 2 * WIDTH + radius + depth]
            if row >= radius:
                beside = beside + now_ref[row - radius]
            if row + radius < rows:
                beside = beside + now_ref[row + radius]
            left = jnp.where(lane >= radius, pltpu.roll(centre, radius, 1), 0.0)
            right = jnp.where(lane < width - radius, pltpu.roll(centre, width - radius, 1), 0.0)
            bending = bending + STENCIL[radius] * (beside + (left + right))
        out_ref[row] = 2.0 * centre - prev_ref[row] + courant_ref[row] * (bending + own_ref[row])


def deep_neighbours(cells):
    count = lax.axis_size("depth")
    if count == 2:
        other = lax.ppermute(cells, "depth", [(0, 1), (1, 0)])
        return other, other
    return (
        lax.ppermute(cells, "depth", [(i, i + 1) for i in range(count - 1)]),
        lax.ppermute(cells, "depth", [(i + 1, i) for i in range(count - 1)]),
    )


def on_device(half_span, image, offset_of, background, wave_now, wave_prev, courant):
    groups = lax.axis_size("off")
    own_slab, prev = background[0], wave_prev[0]

    slabs = {}
    for step in range(1, groups):
        slabs[step] = lax.ppermute(
            own_slab, "off", [(i, (i + step) % groups) for i in range(groups)]
        )
    above, below = deep_neighbours(wave_now[0])
    own, held, now, cells = first_source(image, offset_of, own_slab, wave_now[0], half_span)
    rows, depth, width = now.shape

    returned = []
    part = own
    for step in range(1, groups):
        part = source_of(held, cells, slabs[step], now, part, step, groups, half_span)
        back = [(i, (i - step) % groups) for i in range(groups)]
        returned.append(
            lax.ppermute(part.astype(jnp.float16), "off", back).astype(jnp.float32)
        )

    base = pl.pallas_call(
        step_kernel,
        out_shape=jax.ShapeDtypeStruct(now.shape, jnp.float32),
        in_specs=[VMEM] * 6,
        out_specs=VMEM,
        scratch_shapes=[pltpu.VMEM((rows, depth + 4 * WIDTH, width), jnp.float32)],
        compiler_params=pltpu.CompilerParams(vmem_limit_bytes=32 * MIB),
        cost_estimate=COST,
    )(now, above, below, prev, courant, own)

    after, before = returned[0][rows : rows + WIDTH], returned[-1][-WIDTH:]
    beside = jnp.concatenate([before, jnp.zeros_like(now), after], axis=0)
    sums = functools.reduce(jnp.add, [part[:rows] for part in returned])
    for radius in range(1, WIDTH + 1):
        sums = sums + STENCIL[radius] * (
            beside[WIDTH - radius : WIDTH - radius + rows]
            + beside[WIDTH + radius : WIDTH + radius + rows]
        )
    return (base + courant * sums)[None]


def solution(mesh):
    def whole(image, offset_of, background, wave_now, wave_prev, courant):
        half_span = offset_of.shape[0] // 2
        assert half_span < LANES and background.shape[-1] % LANES == 0
        return jax.shard_map(
            functools.partial(on_device, half_span),
            mesh=mesh,
            in_specs=(
                P("off", None, "depth", None),
                P("off"),
                P(("parts", "shot"), "off", "depth", None),
                P(("parts", "shot"), "off", "depth", None),
                P(("parts", "shot"), "off", "depth", None),
                P("off", "depth", None),
            ),
            out_specs=P(("parts", "shot"), "off", "depth", None),
            check_vma=False,
        )(image, offset_of, background, wave_now, wave_prev, courant)

    return whole
```

time: 34.4 us -> 23.2 us (0.67)
  starting transfers between devices: 17.1 us -> 11 us
  local copies, waits for them, and re-layouts: 5.05 us -> 0.03 us
  waiting for transfers between devices: 4.8 us -> 5.69 us
  other arithmetic: 1.67 us -> 0.8 us
    ppermute x6 -> x4, starting transfers between devices: 11 us -> 4.02 us  [the longest x3 2.53 us: on_device(): lax.ppermute(part.astype(jnp.float16), 'off', back).astype(jnp.float32)]
    unnamed x16 -> x4, local copies, waits for them, and re-layouts: 5.04 us -> 0.01 us
    ppermute x3, starting transfers between devices: 6.06 us -> 6.96 us  [on_device(): lax.ppermute(own_slab, 'off', [(i, (i + step) % groups) for i in range(gr...]
    ppermute x6 -> x4, waiting for transfers between devices: 4.79 us -> 5.69 us  [the longest x3 5.68 us: on_device(): lax.ppermute(part.astype(jnp.float16), 'off', back).astype(jnp.float32)]
    select_n x1 -> x0, other arithmetic: 0.88 us -> none  [neighbour_layers(): jnp.where(here == 0, tail, head)]
    pallas_call x4, Pallas kernels: 4.5 us -> 5.01 us  [the longest x1 3.69 us: first_source(): pl.pallas_call(functools.partial(first_kernel, half_span), out_shape=(plt...]
    pallas_call x1, Pallas kernels: 0.91 us -> 0.44 us  [on_device(): pl.pallas_call(step_kernel, out_shape=jax.ShapeDtypeStruct(now.shape, jnp...]
  transfers between devices with their start and end apart: 9 -> 7, of which waited for: 1 -> 3; matrix products, arithmetic and copies ran while one was open for 3% -> 0% of each run, Pallas kernels for 16% -> 24%
where the time goes in v2:
time: 23.2 us; the launch traced here: 23.1 us
  starting transfers between devices  11 us (47%)
  waiting for transfers between devices  5.69 us (25%)
  Pallas kernels  5.46 us (24%)
  other arithmetic  0.8 us (3%)
    ppermute x3, starting transfers between devices, on_device(): lax.ppermute(own_slab, 'off', [(i, (i + step) % groups) for i in range(gr...  6.96 us
    ppermute x3, waiting for transfers between devices, on_device(): lax.ppermute(part.astype(jnp.float16), 'off', back).astype(jnp.float32)  5.68 us
    pallas_call x1, Pallas kernels, first_source(): pl.pallas_call(functools.partial(first_kernel, half_span), out_shape=(plt...  3.69 us
    ppermute x3, starting transfers between devices, on_device(): lax.ppermute(part.astype(jnp.float16), 'off', back).astype(jnp.float32)  2.53 us
    ppermute x1, starting transfers between devices, deep_neighbours(): other = lax.ppermute(cells, 'depth', [(0, 1), (1, 0)])  1.49 us
    pallas_call x3, Pallas kernels, source_of(): pl.pallas_call(functools.partial(source_kernel, half_span, step, groups),...  1.32 us
    broadcast_in_dim x1, other arithmetic, on_device(): return (base + courant * sums)[None]  0.72 us
  transfers between devices with their start and end apart: 7, of which 3 were waited for; matrix products, arithmetic and copies ran while one was open for 0% of the time, Pallas kernels for 24%

profile of v2, /device:TPU:0, one launch (start us, length us, event | category | flops | bytes accessed | tf_op | source)
XLA Modules:
  0.0 23.1 jit_solution(11270967520260911155)
XLA Ops:
  0.0 3.0 %collective-permute-start.1 = (bf16[8,16,256]{2,1,0:T(8,128)(2,1)}, bf16[8,16,256]{2,1,0:T(8,128)(2,1)S(1)}, u32[]{:S(2)}, u32[]{:S(2)}) collective-permute-start(bf16[8,16,256]{2,1,0:T(8,128)(2,1)} %bitcast.8), channel_id=1, source_target_pairs={{0,4},{4,8},{8,12},{12,0},{1,5},{5,9},{9,13},{13,1},{2,6},{6,10},{... | collective-permute-start | bytes 196616 | tf_op jit(solution)/shard_map/ppermute | solution.py:173
  3.0 2.6 %collective-permute-start.3 = (bf16[8,16,256]{2,1,0:T(8,128)(2,1)}, bf16[8,16,256]{2,1,0:T(8,128)(2,1)S(1)}, u32[]{:S(2)}, u32[]{:S(2)}) collective-permute-start(bf16[8,16,256]{2,1,0:T(8,128)(2,1)} %bitcast.9), channel_id=1, source_target_pairs={{0,8},{4,12},{8,0},{12,4},{1,9},{5,13},{9,1},{13,5},{2,10},{6,14},... | collective-permute-start | bytes 196616 | tf_op jit(solution)/shard_map/ppermute | solution.py:173
  5.6 1.3 %collective-permute-start.5 = (bf16[8,16,256]{2,1,0:T(8,128)(2,1)}, bf16[8,16,256]{2,1,0:T(8,128)(2,1)S(1)}, u32[]{:S(2)}, u32[]{:S(2)}) collective-permute-start(bf16[8,16,256]{2,1,0:T(8,128)(2,1)} %bitcast.10), channel_id=1, source_target_pairs={{0,12},{4,0},{8,4},{12,8},{1,13},{5,1},{9,5},{13,9},{2,14},{6,2},{... | collective-permute-start | bytes 196616 | tf_op jit(solution)/shard_map/ppermute | solution.py:173
  7.0 1.5 %collective-permute-start = (f32[8,16,256]{2,1,0:T(8,128)}, f32[8,16,256]{2,1,0:T(8,128)S(1)}, u32[]{:S(2)}, u32[]{:S(2)}) collective-permute-start(f32[8,16,256]{2,1,0:T(8,128)} %bitcast.6), channel_id=1, source_target_pairs={{0,2},{2,0},{1,3},{3,1},{4,6},{6,4},{5,7},{7,5},{8,10},{10,8},{9,1... | collective-permute-start | bytes 393224 | tf_op jit(solution)/shard_map/ppermute | solution.py:159
  8.5 3.7 %shard_map.64 = (f32[8,16,256]{2,1,0:T(8,128)S(1)}, bf16[16,32,16,256]{3,2,1,0:T(8,128)(2,1)S(1)}, f32[8,16,256]{2,1,0:T(8,128)S(1)}, s32[16]{0:T(128)S(4)}) custom-call(s32[16]{0:T(128)} %offset_ref.1, bf16[16,32,16,256]{3,2,1,0:T(8,128)(2,1)} %image_ref.1, bf16[8,16,256]{2,1,0:T(8,128)(2,1)} %bitcast.11, f32[8,16,256]{2,1,0:T(8,128)} %bitcast.7), custom_call_target="tpu_custom_call" | custom-call | flops 1000 | bytes 1000 | tf_op jit(solution)/shard_map/pallas_call | solution.py:71
  12.2 0.0 collective-permute-done.1.background_ref
  12.2 0.4 %shard_map.66.earlier_ref = f32[12,16,256]{2,1,0:T(8,128)S(1)} custom-call(s32[16]{0:T(128)S(4)} %get-tuple-element.11.offset_ref, bf16[16,32,16,256]{3,2,1,0:T(8,128)(2,1)S(1)} %get-tuple-element.12.image_ref, bf16[8,16,256]{2,1,0:T(8,128)(2,1)S(1)} %collective-permute-done.1.background_ref, f32[8,16,256]{2,1,0:T(8,128)S(1)} %get-tuple-element.9.now_ref, ...), custom_call_target="tpu_custom_call" | custom-call | flops 1000 | bytes 1000 | tf_op jit(solution)/shard_map/pallas_call | solution.py:119
  12.6 0.0 copy-start
  12.7 0.0 copy-start.1
  12.7 0.5 %collective-permute-start.2 = (f16[12,16,256]{2,1,0:T(8,128)(2,1)S(1)}, f16[12,16,256]{2,1,0:T(8,128)(2,1)S(1)}, u32[]{:S(2)}, u32[]{:S(2)}) collective-permute-start(f16[12,16,256]{2,1,0:T(8,128)(2,1)S(1)} %convert_element_type.18), channel_id=1, source_target_pairs={{0,12},{4,0},{8,4},{12,8},{1,13},{5,1},{9,5},{13,9},{2,14},{6,2},{... | collective-permute-start | bytes 294920 | tf_op jit(solution)/shard_map/ppermute | solution.py:186
  13.2 0.0 collective-permute-done.3.background_ref
  13.2 0.4 %shard_map.67.earlier_ref = f32[8,16,256]{2,1,0:T(8,128)S(1)} custom-call(s32[16]{0:T(128)S(4)} %get-tuple-element.11.offset_ref, bf16[16,32,16,256]{3,2,1,0:T(8,128)(2,1)S(1)} %get-tuple-element.12.image_ref, bf16[8,16,256]{2,1,0:T(8,128)(2,1)S(1)} %collective-permute-done.3.background_ref, f32[8,16,256]{2,1,0:T(8,128)S(1)} %get-tuple-element.9.now_ref, ...), custom_call_target="tpu_custom_call" | custom-call | flops 1000 | bytes 1000 | tf_op jit(solution)/shard_map/pallas_call | solution.py:119
  13.6 0.0 collective-permute-done.5.background_ref
  13.6 0.4 %shard_map.68 = f32[12,16,256]{2,1,0:T(8,128)S(1)} custom-call(s32[16]{0:T(128)S(4)} %get-tuple-element.11.offset_ref, bf16[16,32,16,256]{3,2,1,0:T(8,128)(2,1)S(1)} %get-tuple-element.12.image_ref, bf16[8,16,256]{2,1,0:T(8,128)(2,1)S(1)} %collective-permute-done.5.background_ref, f32[8,16,256]{2,1,0:T(8,128)S(1)} %get-tuple-element.9.now_ref, ...), custom_call_target="tpu_custom_call" | custom-call | flops 1000 | bytes 1000 | tf_op jit(solution)/shard_map/pallas_call | solution.py:119
  14.1 1.6 %collective-permute-start.6 = (f16[12,16,256]{2,1,0:T(8,128)(2,1)S(1)}, f16[12,16,256]{2,1,0:T(8,128)(2,1)S(1)}, u32[]{:S(2)}, u32[]{:S(2)}) collective-permute-start(f16[12,16,256]{2,1,0:T(8,128)(2,1)S(1)} %convert_element_type.22), channel_id=1, source_target_pairs={{0,4},{4,8},{8,12},{12,0},{1,5},{5,9},{9,13},{13,1},{2,6},{6,10},{... | collective-permute-start | bytes 294920 | tf_op jit(solution)/shard_map/ppermute | solution.py:186
  15.7 0.4 %collective-permute-start.4 = (f16[8,16,256]{2,1,0:T(8,128)(2,1)S(1)}, f16[8,16,256]{2,1,0:T(8,128)(2,1)S(1)}, u32[]{:S(2)}, u32[]{:S(2)}) collective-permute-start(f16[8,16,256]{2,1,0:T(8,128)(2,1)S(1)} %convert_element_type.20), channel_id=1, source_target_pairs={{0,8},{4,12},{8,0},{12,4},{1,9},{5,13},{9,1},{13,5},{2,10},{6,14},... | collective-permute-start | bytes 196616 | tf_op jit(solution)/shard_map/ppermute | solution.py:186
  16.1 0.0 collective-permute-done.above_ref.below_ref
  16.2 0.0 copy-done
  16.2 0.0 copy-done.1
  16.2 0.4 %shard_map.65 = f32[8,16,256]{2,1,0:T(8,128)S(1)} custom-call(f32[8,16,256]{2,1,0:T(8,128)S(1)} %get-tuple-element.9.now_ref, f32[8,16,256]{2,1,0:T(8,128)S(1)} %collective-permute-done.above_ref.below_ref, f32[8,16,256]{2,1,0:T(8,128)S(1)} %collective-permute-done.above_ref.below_ref, f32[8,16,256]{2,1,0:T(8,128)S(1)} %bitcast.5, ...), custom_call_target="tpu_custom_call" | custom-call | flops 1000 | bytes 1000 | tf_op jit(solution)/shard_map/pallas_call | solution.py:189
  16.6 1.8 %collective-permute-done.2 = f16[12,16,256]{2,1,0:T(8,128)(2,1)S(1)} collective-permute-done((f16[12,16,256]{2,1,0:T(8,128)(2,1)S(1)}, f16[12,16,256]{2,1,0:T(8,128)(2,1)S(1)}, u32[]{:S(2)}, u32[]{:S(2)}) %collective-permute-start.2) | collective-permute-done | bytes 98336 | tf_op jit(solution)/shard_map/ppermute | solution.py:186
  18.4 2.2 %collective-permute-done.6 = f16[12,16,256]{2,1,0:T(8,128)(2,1)S(1)} collective-permute-done((f16[12,16,256]{2,1,0:T(8,128)(2,1)S(1)}, f16[12,16,256]{2,1,0:T(8,128)(2,1)S(1)}, u32[]{:S(2)}, u32[]{:S(2)}) %collective-permute-start.6) | collective-permute-done | bytes 98336 | tf_op jit(solution)/shard_map/ppermute | solution.py:186
  20.7 1.7 %collective-permute-done.4 = f16[8,16,256]{2,1,0:T(8,128)(2,1)S(1)} collective-permute-done((f16[8,16,256]{2,1,0:T(8,128)(2,1)S(1)}, f16[8,16,256]{2,1,0:T(8,128)(2,1)S(1)}, u32[]{:S(2)}, u32[]{:S(2)}) %collective-permute-start.4) | collective-permute-done | bytes 65568 | tf_op jit(solution)/shard_map/ppermute | solution.py:186
  22.4 0.7 %fusion.8 = f32[1,8,16,256]{3,2,1,0:T(8,128)} fusion(f32[8,16,256]{2,1,0:T(8,128)S(1)} %shard_map.65, f32[8,16,256]{2,1,0:T(8,128)S(1)} %copy-done, f32[4,16,256]{2,1,0:T(8,128)S(1)} %slice.58, f32[4,16,256]{2,1,0:T(8,128)S(1)} %slice.59, f32[12,16,256]{2,1,0:T(8,128)S(1)} %convert_element_type.23, f32[12,16,256]{2,1,0:T(8,128)S(1)} %convert_element_type.19, ...), kind=kLoop, calls=%fused_computation.16 | loop fusion | flops 557056 | bytes 851968 | tf_op jit(solution)/shard_map/broadcast_in_dim | solution.py:207
  (7 shorter events, 0.1 us)
Async XLA Ops:
  0.0 12.2 %collective-permute-start.1 = (bf16[8,16,256]{2,1,0:T(8,128)(2,1)}, bf16[8,16,256]{2,1,0:T(8,128)(2,1)S(1)}, u32[]{:S(2)}, u32[]{:S(2)}) collective-permute-start(bf16[8,16,256]{2,1,0:T(8,128)(2,1)} %bitcast.8), channel_id=1, source_target_pairs={{0,4},{4,8},{8,12},{12,0},{1,5},{5,9},{9,13},{13,1},{2,6},{6,10},{... | collective-permute-start | bytes 196616 | tf_op jit(solution)/shard_map/ppermute | solution.py:173
  3.0 10.1 %collective-permute-start.3 = (bf16[8,16,256]{2,1,0:T(8,128)(2,1)}, bf16[8,16,256]{2,1,0:T(8,128)(2,1)S(1)}, u32[]{:S(2)}, u32[]{:S(2)}) collective-permute-start(bf16[8,16,256]{2,1,0:T(8,128)(2,1)} %bitcast.9), channel_id=1, source_target_pairs={{0,8},{4,12},{8,0},{12,4},{1,9},{5,13},{9,1},{13,5},{2,10},{6,14},... | collective-permute-start | bytes 196616 | tf_op jit(solution)/shard_map/ppermute | solution.py:173
  5.6 8.0 %collective-permute-start.5 = (bf16[8,16,256]{2,1,0:T(8,128)(2,1)}, bf16[8,16,256]{2,1,0:T(8,128)(2,1)S(1)}, u32[]{:S(2)}, u32[]{:S(2)}) collective-permute-start(bf16[8,16,256]{2,1,0:T(8,128)(2,1)} %bitcast.10), channel_id=1, source_target_pairs={{0,12},{4,0},{8,4},{12,8},{1,13},{5,1},{9,5},{13,9},{2,14},{6,2},{... | collective-permute-start | bytes 196616 | tf_op jit(solution)/shard_map/ppermute | solution.py:173
  7.0 9.2 %collective-permute-start = (f32[8,16,256]{2,1,0:T(8,128)}, f32[8,16,256]{2,1,0:T(8,128)S(1)}, u32[]{:S(2)}, u32[]{:S(2)}) collective-permute-start(f32[8,16,256]{2,1,0:T(8,128)} %bitcast.6), channel_id=1, source_target_pairs={{0,2},{2,0},{1,3},{3,1},{4,6},{6,4},{5,7},{7,5},{8,10},{10,8},{9,1... | collective-permute-start | bytes 393224 | tf_op jit(solution)/shard_map/ppermute | solution.py:159
  12.6 3.5 %copy-start = (f32[8,16,256]{2,1,0:T(8,128)S(1)}, f32[8,16,256]{2,1,0:T(8,128)}, u32[]{:S(2)}) copy-start(f32[8,16,256]{2,1,0:T(8,128)} %courant_ref.1) | copy-start | bytes 393220
  12.7 3.5 %copy-start.1 = (f32[1,8,16,256]{3,2,1,0:T(8,128)S(1)}, f32[1,8,16,256]{3,2,1,0:T(8,128)}, u32[]{:S(2)}) copy-start(f32[1,8,16,256]{3,2,1,0:T(8,128)} %param.10) | copy-start | bytes 393220
  12.7 5.7 %collective-permute-start.2 = (f16[12,16,256]{2,1,0:T(8,128)(2,1)S(1)}, f16[12,16,256]{2,1,0:T(8,128)(2,1)S(1)}, u32[]{:S(2)}, u32[]{:S(2)}) collective-permute-start(f16[12,16,256]{2,1,0:T(8,128)(2,1)S(1)} %convert_element_type.18), channel_id=1, source_target_pairs={{0,12},{4,0},{8,4},{12,8},{1,13},{5,1},{9,5},{13,9},{2,14},{6,2},{... | collective-permute-start | bytes 294920 | tf_op jit(solution)/shard_map/ppermute | solution.py:186
  14.1 6.6 %collective-permute-start.6 = (f16[12,16,256]{2,1,0:T(8,128)(2,1)S(1)}, f16[12,16,256]{2,1,0:T(8,128)(2,1)S(1)}, u32[]{:S(2)}, u32[]{:S(2)}) collective-permute-start(f16[12,16,256]{2,1,0:T(8,128)(2,1)S(1)} %convert_element_type.22), channel_id=1, source_target_pairs={{0,4},{4,8},{8,12},{12,0},{1,5},{5,9},{9,13},{13,1},{2,6},{6,10},{... | collective-permute-start | bytes 294920 | tf_op jit(solution)/shard_map/ppermute | solution.py:186
  15.7 6.6 %collective-permute-start.4 = (f16[8,16,256]{2,1,0:T(8,128)(2,1)S(1)}, f16[8,16,256]{2,1,0:T(8,128)(2,1)S(1)}, u32[]{:S(2)}, u32[]{:S(2)}) collective-permute-start(f16[8,16,256]{2,1,0:T(8,128)(2,1)S(1)} %convert_element_type.20), channel_id=1, source_target_pairs={{0,8},{4,12},{8,0},{12,4},{1,9},{5,13},{9,1},{13,5},{2,10},{6,14},... | collective-permute-start | bytes 196616 | tf_op jit(solution)/shard_map/ppermute | solution.py:186

commit v3 on v2

v3 whole, which is shorter than its diff:
```python
import functools

import jax
import jax.numpy as jnp
from jax import lax
from jax.experimental import pallas as pl
from jax.experimental.pallas import tpu as pltpu
from jax.sharding import PartitionSpec as P

STENCIL = (-205.0 / 72.0, 8.0 / 5.0, -1.0 / 5.0, 8.0 / 315.0, -1.0 / 560.0)
WIDTH = len(STENCIL) - 1
LANES = 128
MIB = 2**20

VMEM = pl.BlockSpec(memory_space=pltpu.VMEM)
SMEM = pl.BlockSpec(memory_space=pltpu.SMEM)
ANY = pl.BlockSpec(memory_space=pl.ANY)
COST = pl.CostEstimate(flops=1000, bytes_accessed=1000, transcendentals=0)


def add_column(half_span, offset_ref, image_ref, background_ref, first_row, column, running):
    rows, depth, width = background_ref.shape
    cells = offset_ref[column] - half_span
    back = cells < 0
    turn = jnp.where(back, cells + LANES, cells)
    wrapped = lax.broadcasted_iota(jnp.int32, (depth, LANES), 1) < turn
    result = []
    for row in range(rows):
        turned = [
            pltpu.roll(background_ref[row, :, start : start + LANES], turn, 1)
            for start in range(0, width, LANES)
        ]
        zero = jnp.zeros_like(turned[0])
        ahead = [zero] + turned
        behind = turned + [zero]
        chosen = [jnp.where(back, b, a) for a, b in zip(ahead, behind)]
        shifted = [jnp.where(wrapped, a, b) for a, b in zip(chosen[:-1], chosen[1:])]
        factor = image_ref[column, first_row + row].astype(jnp.float32)
        result.append(running[row] + factor * jnp.concatenate(shifted, 1).astype(jnp.float32))
    return tuple(result)


def slab_sums(half_span, offset_ref, image_ref, background_ref, slab):
    rows, depth, width = background_ref.shape
    add = functools.partial(
        add_column, half_span, offset_ref, image_ref, background_ref, slab * rows
    )
    totals = (jnp.zeros((depth, width), jnp.float32),) * rows
    for column in range(image_ref.shape[0]):
        totals = add(column, totals)
    return totals


def move_kernel(*refs):
    count = (len(refs) - 1) // 2
    arrived = refs[-1]
    copies = [
        pltpu.make_async_copy(refs[i], refs[count + i], arrived.at[i]) for i in range(count)
    ]
    for copy in copies:
        copy.start()
    for copy in copies:
        copy.wait()


def moved(*pairs):
    return pl.pallas_call(
        move_kernel,
        out_shape=[space(x.shape, x.dtype) for x, space in pairs],
        in_specs=[ANY] * len(pairs),
        out_specs=[pl.BlockSpec(memory_space=space) for _, space in pairs],
        scratch_shapes=[pltpu.SemaphoreType.DMA((len(pairs),))],
        compiler_params=pltpu.CompilerParams(vmem_limit_bytes=32 * MIB),
        cost_estimate=COST,
    )(*[pltpu.with_memory_space_constraint(x, pltpu.HBM) for x, _ in pairs])


def source_kernel(half_span, step, groups, offset_ref, image_ref, background_ref, now_ref, earlier_ref, out_ref, *edge_refs):
    del earlier_ref
    rows, depth, width = background_ref.shape
    here = lax.axis_index("off")
    slab = lax.rem(here - step + groups, groups)
    totals = slab_sums(half_span, offset_ref, image_ref, background_ref, slab)
    for row in range(rows):
        out_ref[row] = totals[row]
    at = rows
    if step == 1:
        for layer in range(WIDTH):
            out_ref[at + layer] = jnp.where(here != 0, now_ref[layer], 0.0)
        at += WIDTH
    if step == groups - 1:
        for layer in range(WIDTH):
            out_ref[at + layer] = jnp.where(
                here != groups - 1, now_ref[rows - WIDTH + layer], 0.0
            )
    if len(edge_refs) == 1:
        at_top = lax.axis_index("depth") == 0
        for row in range(rows):
            edge_refs[0][row] = jnp.where(
                at_top, now_ref[row, depth - WIDTH :], now_ref[row, :WIDTH]
            )
    elif edge_refs:
        for row in range(rows):
            edge_refs[0][row] = now_ref[row, depth - WIDTH :]
            edge_refs[1][row] = now_ref[row, :WIDTH]


def source_of(image, offset_of, background, now, earlier, step, groups, half_span, edges):
    rows, depth, width = background.shape
    extra = WIDTH * ((step == 1) + (step == groups - 1))
    return pl.pallas_call(
        functools.partial(source_kernel, half_span, step, groups),
        out_shape=[pltpu.VMEM((rows + extra, depth, width), jnp.float32)]
        + [pltpu.VMEM((rows, WIDTH, width), now.dtype)] * edges,
        in_specs=[SMEM, VMEM, VMEM, VMEM, ANY],
        out_specs=[VMEM] * (1 + edges),
        compiler_params=pltpu.CompilerParams(vmem_limit_bytes=32 * MIB),
        cost_estimate=COST,
    )(offset_of, image, background, now, earlier)


def step_kernel(half_span, offset_ref, image_ref, background_ref, now_ref, above_ref, below_ref, prev_ref, courant_ref, out_ref, deep_ref):
    rows, depth, width = now_ref.shape
    at = lax.axis_index("depth")
    deep_ref[:, 2 * WIDTH : 2 * WIDTH + depth] = now_ref[...]
    deep_ref[:, WIDTH : 2 * WIDTH] = jnp.where(
        at != 0, above_ref[...], 0.0
    )
    deep_ref[:, 2 * WIDTH + depth : 3 * WIDTH + depth] = jnp.where(
        at != lax.axis_size("depth") - 1, below_ref[...], 0.0
    )
    lane = lax.broadcasted_iota(jnp.int32, (depth, width), 1)
    own = slab_sums(half_span, offset_ref, image_ref, background_ref, lax.axis_index("off"))
    for row in range(rows):
        centre = now_ref[row]
        bending = 3.0 * STENCIL[0] * centre
        for radius in range(1, WIDTH + 1):
            beside = deep_ref[row, 2 * WIDTH - radius : 2 * WIDTH - radius + depth]
            beside = beside + deep_ref[row, 2 * WIDTH + radius : 2 * WIDTH + radius + depth]
            if row >= radius:
                beside = beside + now_ref[row - radius]
            if row + radius < rows:
                beside = beside + now_ref[row + radius]
            left = jnp.where(lane >= radius, pltpu.roll(centre, radius, 1), 0.0)
            right = jnp.where(lane < width - radius, pltpu.roll(centre, width - radius, 1), 0.0)
            bending = bending + STENCIL[radius] * (beside + (left + right))
        out_ref[row] = 2.0 * centre - prev_ref[row] + courant_ref[row] * (bending + own[row])


def deep_layers(edges):
    count = lax.axis_size("depth")
    if count == 2:
        other = lax.ppermute(edges[0], "depth", [(0, 1), (1, 0)])
        return other, other
    return (
        lax.ppermute(edges[0], "depth", [(i, i + 1) for i in range(count - 1)]),
        lax.ppermute(edges[1], "depth", [(i + 1, i) for i in range(count - 1)]),
    )


def on_device(half_span, image, offset_of, background, wave_now, wave_prev, courant):
    groups = lax.axis_size("off")
    own_slab, prev = background[0], wave_prev[0]

    slabs = {}
    order = sorted(range(1, groups), key=lambda step: min(step, groups - step))
    for step in order:
        slabs[step] = lax.ppermute(
            own_slab, "off", [(i, (i + step) % groups) for i in range(groups)]
        )
    held, now, cells, own_slab = moved(
        (image, pltpu.VMEM),
        (wave_now[0], pltpu.VMEM),
        (offset_of, pltpu.SMEM),
        (own_slab, pltpu.VMEM),
    )
    rows, depth, width = now.shape

    returned = {}
    part = now
    for step in order:
        edges = 0 if step != order[0] else 1 if lax.axis_size("depth") == 2 else 2
        part, *rest = source_of(
            held, cells, slabs[step], now, part, step, groups, half_span, edges
        )
        if edges:
            above, below = deep_layers(rest)
        back = [(i, (i - step) % groups) for i in range(groups)]
        returned[step] = lax.ppermute(part.astype(jnp.float16), "off", back).astype(jnp.float32)
    returned = [returned[step] for step in range(1, groups)]

    base = pl.pallas_call(
        functools.partial(step_kernel, half_span),
        out_shape=jax.ShapeDtypeStruct(now.shape, jnp.float32),
        in_specs=[SMEM] + [VMEM] * 7,
        out_specs=VMEM,
        scratch_shapes=[pltpu.VMEM((rows, depth + 4 * WIDTH, width), jnp.float32)],
        compiler_params=pltpu.CompilerParams(vmem_limit_bytes=32 * MIB),
        cost_estimate=COST,
    )(cells, held, own_slab, now, above, below, prev, courant)

    after, before = returned[0][rows : rows + WIDTH], returned[-1][-WIDTH:]
    beside = jnp.concatenate([before, jnp.zeros_like(now), after], axis=0)
    sums = functools.reduce(jnp.add, [part[:rows] for part in returned])
    for radius in range(1, WIDTH + 1):
        sums = sums + STENCIL[radius] * (
            beside[WIDTH - radius : WIDTH - radius + rows]
            + beside[WIDTH + radius : WIDTH + radius + rows]
        )
    return (base + courant * sums)[None]


def solution(mesh):
    def whole(image, offset_of, background, wave_now, wave_prev, courant):
        half_span = offset_of.shape[0] // 2
        assert half_span < LANES and background.shape[-1] % LANES == 0
        return jax.shard_map(
            functools.partial(on_device, half_span),
            mesh=mesh,
            in_specs=(
                P("off", None, "depth", None),
                P("off"),
                P(("parts", "shot"), "off", "depth", None),
                P(("parts", "shot"), "off", "depth", None),
                P(("parts", "shot"), "off", "depth", None),
                P("off", "depth", None),
            ),
            out_specs=P(("parts", "shot"), "off", "depth", None),
            check_vma=False,
        )(image, offset_of, background, wave_now, wave_prev, courant)

    return whole
```

time: 23.2 us -> 20.6 us (0.89)
  waiting for transfers between devices: 5.69 us -> 3.2 us
  Pallas kernels: 5.46 us -> 4.41 us
  starting transfers between devices: 11 us -> 11.9 us
    ppermute x3, waiting for transfers between devices: 5.68 us -> 0.99 us  [on_device(): lax.ppermute(part.astype(jnp.float16), 'off', back).astype(jnp.float32)]
    ppermute x1, waiting for transfers between devices: 0.01 us -> 2.2 us  [deep_layers(): other = lax.ppermute(edges[0], 'depth', [(0, 1), (1, 0)])]
    ppermute x3, starting transfers between devices: 2.53 us -> 4.11 us  [on_device(): lax.ppermute(part.astype(jnp.float16), 'off', back).astype(jnp.float32)]
    pallas_call x2, Pallas kernels: 4.14 us -> 3.08 us  [the longest x1 2.23 us: moved(): pl.pallas_call(move_kernel, out_shape=[space(x.shape, x.dtype) for x, spa...]
    ppermute x3, starting transfers between devices: 6.96 us -> 6.06 us  [on_device(): lax.ppermute(own_slab, 'off', [(i, (i + step) % groups) for i in range(gr...]
  transfers between devices with their start and end apart: 7 -> 7, of which waited for: 3 -> 2; matrix products, arithmetic and copies ran while one was open for 0% -> 0% of each run, Pallas kernels for 24% -> 22%
where the time goes in v3:
time: 20.6 us; the launch traced here: 20.5 us
  starting transfers between devices  11.9 us (58%)
  Pallas kernels  4.41 us (21%)
  waiting for transfers between devices  3.2 us (16%)
  other arithmetic  0.8 us (4%)
    ppermute x3, starting transfers between devices, on_device(): lax.ppermute(own_slab, 'off', [(i, (i + step) % groups) for i in range(gr...  6.06 us
    ppermute x3, starting transfers between devices, on_device(): lax.ppermute(part.astype(jnp.float16), 'off', back).astype(jnp.float32)  4.11 us
    pallas_call x1, Pallas kernels, moved(): pl.pallas_call(move_kernel, out_shape=[space(x.shape, x.dtype) for x, spa...  2.23 us
    ppermute x1, waiting for transfers between devices, deep_layers(): other = lax.ppermute(edges[0], 'depth', [(0, 1), (1, 0)])  2.2 us
    ppermute x1, starting transfers between devices, deep_layers(): other = lax.ppermute(edges[0], 'depth', [(0, 1), (1, 0)])  1.71 us
    pallas_call x3, Pallas kernels, source_of(): pl.pallas_call(functools.partial(source_kernel, half_span, step, groups),...  1.33 us
    ppermute x3, waiting for transfers between devices, on_device(): lax.ppermute(part.astype(jnp.float16), 'off', back).astype(jnp.float32)  0.99 us
    pallas_call x1, Pallas kernels, on_device(): pl.pallas_call(functools.partial(step_kernel, half_span), out_shape=jax.S...  0.85 us
  transfers between devices with their start and end apart: 7, of which 2 were waited for; matrix products, arithmetic and copies ran while one was open for 0% of the time, Pallas kernels for 22%

profile of v3, /device:TPU:0, one launch (start us, length us, event | category | flops | bytes accessed | tf_op | source)
XLA Modules:
  0.0 20.5 jit_solution(8827964029417760326)
XLA Ops:
  0.0 3.0 %collective-permute-start = (bf16[8,16,256]{2,1,0:T(8,128)(2,1)}, bf16[8,16,256]{2,1,0:T(8,128)(2,1)S(1)}, u32[]{:S(2)}, u32[]{:S(2)}) collective-permute-start(bf16[8,16,256]{2,1,0:T(8,128)(2,1)} %bitcast.7), channel_id=1, source_target_pairs={{0,4},{4,8},{8,12},{12,0},{1,5},{5,9},{9,13},{13,1},{2,6},{6,10},{... | collective-permute-start | bytes 196616 | tf_op jit(solution)/shard_map/ppermute | solution.py:168
  3.0 2.0 %collective-permute-start.4 = (bf16[8,16,256]{2,1,0:T(8,128)(2,1)}, bf16[8,16,256]{2,1,0:T(8,128)(2,1)S(1)}, u32[]{:S(2)}, u32[]{:S(2)}) collective-permute-start(bf16[8,16,256]{2,1,0:T(8,128)(2,1)} %bitcast.8), channel_id=1, source_target_pairs={{0,12},{4,0},{8,4},{12,8},{1,13},{5,1},{9,5},{13,9},{2,14},{6,2},{... | collective-permute-start | bytes 196616 | tf_op jit(solution)/shard_map/ppermute | solution.py:168
  5.1 1.0 %collective-permute-start.3 = (bf16[8,16,256]{2,1,0:T(8,128)(2,1)}, bf16[8,16,256]{2,1,0:T(8,128)(2,1)S(1)}, u32[]{:S(2)}, u32[]{:S(2)}) collective-permute-start(bf16[8,16,256]{2,1,0:T(8,128)(2,1)} %bitcast.9), channel_id=1, source_target_pairs={{0,8},{4,12},{8,0},{12,4},{1,9},{5,13},{9,1},{13,5},{2,10},{6,14},... | collective-permute-start | bytes 196616 | tf_op jit(solution)/shard_map/ppermute | solution.py:168
  6.1 2.2 %shard_map.64 = (bf16[16,32,16,256]{3,2,1,0:T(8,128)(2,1)S(1)}, f32[8,16,256]{2,1,0:T(8,128)S(1)}, s32[16]{0:T(128)S(4)}, bf16[8,16,256]{2,1,0:T(8,128)(2,1)S(1)}) custom-call(bf16[16,32,16,256]{3,2,1,0:T(8,128)(2,1)} %refs_0_.1, f32[8,16,256]{2,1,0:T(8,128)} %bitcast.6, s32[16]{0:T(128)} %refs_2_.1, bf16[8,16,256]{2,1,0:T(8,128)(2,1)} %bitcast.10), custom_call_target="tpu_custom_call" | custom-call | flops 1000 | bytes 1000 | tf_op jit(solution)/shard_map/pallas_call | solution.py:67
  8.3 0.0 collective-permute-done.background_ref
  8.3 0.5 %shard_map.65 = (f32[12,16,256]{2,1,0:T(8,128)S(1)}, f32[8,4,256]{2,1,0:T(4,128)S(1)}) custom-call(s32[16]{0:T(128)S(4)} %get-tuple-element.11.offset_ref, bf16[16,32,16,256]{3,2,1,0:T(8,128)(2,1)S(1)} %get-tuple-element.12.image_ref, bf16[8,16,256]{2,1,0:T(8,128)(2,1)S(1)} %collective-permute-done.background_ref, ...), custom_call_target="tpu_custom_call" | custom-call | flops 1000 | bytes 1000 | tf_op jit(solution)/shard_map/pallas_call | solution.py:111
  8.8 0.0 collective-permute-done.4.background_ref
  8.8 0.0 copy-start
  8.8 0.0 copy-start.1
  8.8 0.4 %shard_map.67.earlier_ref = f32[12,16,256]{2,1,0:T(8,128)S(1)} custom-call(s32[16]{0:T(128)S(4)} %get-tuple-element.11.offset_ref, bf16[16,32,16,256]{3,2,1,0:T(8,128)(2,1)S(1)} %get-tuple-element.12.image_ref, bf16[8,16,256]{2,1,0:T(8,128)(2,1)S(1)} %collective-permute-done.4.background_ref, f32[8,16,256]{2,1,0:T(8,128)S(1)} %get-tuple-element.14.now_ref.earlier_ref, ...), custom_call_target="tpu_custom_call" | custom-call | flops 1000 | bytes 1000 | tf_op jit(solution)/shard_map/pallas_call | solution.py:111
  9.3 2.4 %collective-permute-start.6 = (f16[12,16,256]{2,1,0:T(8,128)(2,1)S(1)}, f16[12,16,256]{2,1,0:T(8,128)(2,1)S(1)}, u32[]{:S(2)}, u32[]{:S(2)}) collective-permute-start(f16[12,16,256]{2,1,0:T(8,128)(2,1)S(1)} %convert_element_type.22), channel_id=1, source_target_pairs={{0,4},{4,8},{8,12},{12,0},{1,5},{5,9},{9,13},{13,1},{2,6},{6,10},{... | collective-permute-start | bytes 294920 | tf_op jit(solution)/shard_map/ppermute | solution.py:189
  11.7 1.5 %collective-permute-start.2 = (f16[12,16,256]{2,1,0:T(8,128)(2,1)S(1)}, f16[12,16,256]{2,1,0:T(8,128)(2,1)S(1)}, u32[]{:S(2)}, u32[]{:S(2)}) collective-permute-start(f16[12,16,256]{2,1,0:T(8,128)(2,1)S(1)} %convert_element_type.18), channel_id=1, source_target_pairs={{0,12},{4,0},{8,4},{12,8},{1,13},{5,1},{9,5},{13,9},{2,14},{6,2},{... | collective-permute-start | bytes 294920 | tf_op jit(solution)/shard_map/ppermute | solution.py:189
  13.2 0.0 collective-permute-done.3.background_ref
  13.2 0.4 %shard_map.68 = f32[8,16,256]{2,1,0:T(8,128)S(1)} custom-call(s32[16]{0:T(128)S(4)} %get-tuple-element.11.offset_ref, bf16[16,32,16,256]{3,2,1,0:T(8,128)(2,1)S(1)} %get-tuple-element.12.image_ref, bf16[8,16,256]{2,1,0:T(8,128)(2,1)S(1)} %collective-permute-done.3.background_ref, f32[8,16,256]{2,1,0:T(8,128)S(1)} %get-tuple-element.14.now_ref.earlier_ref, ...), custom_call_target="tpu_custom_call" | custom-call | flops 1000 | bytes 1000 | tf_op jit(solution)/shard_map/pallas_call | solution.py:111
  13.7 0.2 collective-permute-start.5
  13.9 1.7 %collective-permute-start.1 = (f32[8,4,256]{2,1,0:T(4,128)S(1)}, f32[8,4,256]{2,1,0:T(4,128)S(1)}, u32[]{:S(2)}, u32[]{:S(2)}) collective-permute-start(f32[8,4,256]{2,1,0:T(4,128)S(1)} %get-tuple-element.15), channel_id=1, source_target_pairs={{0,2},{2,0},{1,3},{3,1},{4,6},{6,4},{5,7},{7,5},{8,10},{10,8},{9,1... | collective-permute-start | bytes 98312 | tf_op jit(solution)/shard_map/ppermute | solution.py:153
  15.6 2.2 %collective-permute-done.1.above_ref.below_ref = f32[8,4,256]{2,1,0:T(4,128)S(1)} collective-permute-done((f32[8,4,256]{2,1,0:T(4,128)S(1)}, f32[8,4,256]{2,1,0:T(4,128)S(1)}, u32[]{:S(2)}, u32[]{:S(2)}) %collective-permute-start.1) | collective-permute-done | bytes 32800 | tf_op jit(solution)/shard_map/ppermute | solution.py:153
  17.8 0.0 copy-done
  17.8 0.0 copy-done.1
  17.8 0.8 %shard_map.66 = f32[8,16,256]{2,1,0:T(8,128)S(1)} custom-call(s32[16]{0:T(128)S(4)} %get-tuple-element.11.offset_ref, bf16[16,32,16,256]{3,2,1,0:T(8,128)(2,1)S(1)} %get-tuple-element.12.image_ref, bf16[8,16,256]{2,1,0:T(8,128)(2,1)S(1)} %get-tuple-element.13.background_ref, f32[8,16,256]{2,1,0:T(8,128)S(1)} %get-tuple-element.14.now_ref.earlier_ref, ...), custom_call_target="tpu_custom_call" | custom-call | flops 1000 | bytes 1000 | tf_op jit(solution)/shard_map/pallas_call | solution.py:192
  18.7 0.0 collective-permute-done.6
  18.7 0.0 collective-permute-done.2
  18.8 1.0 %collective-permute-done.5 = f16[8,16,256]{2,1,0:T(8,128)(2,1)S(1)} collective-permute-done((f16[8,16,256]{2,1,0:T(8,128)(2,1)S(1)}, f16[8,16,256]{2,1,0:T(8,128)(2,1)S(1)}, u32[]{:S(2)}, u32[]{:S(2)}) %collective-permute-start.5) | collective-permute-done | bytes 65568 | tf_op jit(solution)/shard_map/ppermute | solution.py:189
  19.7 0.7 %fusion.8 = f32[1,8,16,256]{3,2,1,0:T(8,128)} fusion(f32[8,16,256]{2,1,0:T(8,128)S(1)} %shard_map.66, f32[8,16,256]{2,1,0:T(8,128)S(1)} %copy-done, f32[4,16,256]{2,1,0:T(8,128)S(1)} %slice.58, f32[4,16,256]{2,1,0:T(8,128)S(1)} %slice.59, f32[12,16,256]{2,1,0:T(8,128)S(1)} %convert_element_type.23, f32[12,16,256]{2,1,0:T(8,128)S(1)} %convert_element_type.19, ...), kind=kLoop, calls=%fused_computation.16 | loop fusion | flops 557056 | bytes 851968 | tf_op jit(solution)/shard_map/broadcast_in_dim | solution.py:210
  (7 shorter events, 0.1 us)
Async XLA Ops:
  0.0 8.3 %collective-permute-start = (bf16[8,16,256]{2,1,0:T(8,128)(2,1)}, bf16[8,16,256]{2,1,0:T(8,128)(2,1)S(1)}, u32[]{:S(2)}, u32[]{:S(2)}) collective-permute-start(bf16[8,16,256]{2,1,0:T(8,128)(2,1)} %bitcast.7), channel_id=1, source_target_pairs={{0,4},{4,8},{8,12},{12,0},{1,5},{5,9},{9,13},{13,1},{2,6},{6,10},{... | collective-permute-start | bytes 196616 | tf_op jit(solution)/shard_map/ppermute | solution.py:168
  3.0 5.8 %collective-permute-start.4 = (bf16[8,16,256]{2,1,0:T(8,128)(2,1)}, bf16[8,16,256]{2,1,0:T(8,128)(2,1)S(1)}, u32[]{:S(2)}, u32[]{:S(2)}) collective-permute-start(bf16[8,16,256]{2,1,0:T(8,128)(2,1)} %bitcast.8), channel_id=1, source_target_pairs={{0,12},{4,0},{8,4},{12,8},{1,13},{5,1},{9,5},{13,9},{2,14},{6,2},{... | collective-permute-start | bytes 196616 | tf_op jit(solution)/shard_map/ppermute | solution.py:168
  5.1 8.2 %collective-permute-start.3 = (bf16[8,16,256]{2,1,0:T(8,128)(2,1)}, bf16[8,16,256]{2,1,0:T(8,128)(2,1)S(1)}, u32[]{:S(2)}, u32[]{:S(2)}) collective-permute-start(bf16[8,16,256]{2,1,0:T(8,128)(2,1)} %bitcast.9), channel_id=1, source_target_pairs={{0,8},{4,12},{8,0},{12,4},{1,9},{5,13},{9,1},{13,5},{2,10},{6,14},... | collective-permute-start | bytes 196616 | tf_op jit(solution)/shard_map/ppermute | solution.py:168
  8.8 9.0 %copy-start = (f32[8,16,256]{2,1,0:T(8,128)S(1)}, f32[8,16,256]{2,1,0:T(8,128)}, u32[]{:S(2)}) copy-start(f32[8,16,256]{2,1,0:T(8,128)} %courant_ref.1) | copy-start | bytes 393220
  8.8 9.0 %copy-start.1 = (f32[1,8,16,256]{3,2,1,0:T(8,128)S(1)}, f32[1,8,16,256]{3,2,1,0:T(8,128)}, u32[]{:S(2)}) copy-start(f32[1,8,16,256]{3,2,1,0:T(8,128)} %param.10) | copy-start | bytes 393220
  9.3 9.4 %collective-permute-start.6 = (f16[12,16,256]{2,1,0:T(8,128)(2,1)S(1)}, f16[12,16,256]{2,1,0:T(8,128)(2,1)S(1)}, u32[]{:S(2)}, u32[]{:S(2)}) collective-permute-start(f16[12,16,256]{2,1,0:T(8,128)(2,1)S(1)} %convert_element_type.22), channel_id=1, source_target_pairs={{0,4},{4,8},{8,12},{12,0},{1,5},{5,9},{9,13},{13,1},{2,6},{6,10},{... | collective-permute-start | bytes 294920 | tf_op jit(solution)/shard_map/ppermute | solution.py:189
  11.7 7.0 %collective-permute-start.2 = (f16[12,16,256]{2,1,0:T(8,128)(2,1)S(1)}, f16[12,16,256]{2,1,0:T(8,128)(2,1)S(1)}, u32[]{:S(2)}, u32[]{:S(2)}) collective-permute-start(f16[12,16,256]{2,1,0:T(8,128)(2,1)S(1)} %convert_element_type.18), channel_id=1, source_target_pairs={{0,12},{4,0},{8,4},{12,8},{1,13},{5,1},{9,5},{13,9},{2,14},{6,2},{... | collective-permute-start | bytes 294920 | tf_op jit(solution)/shard_map/ppermute | solution.py:189
  13.7 6.0 %collective-permute-start.5 = (f16[8,16,256]{2,1,0:T(8,128)(2,1)S(1)}, f16[8,16,256]{2,1,0:T(8,128)(2,1)S(1)}, u32[]{:S(2)}, u32[]{:S(2)}) collective-permute-start(f16[8,16,256]{2,1,0:T(8,128)(2,1)S(1)} %convert_element_type.20), channel_id=1, source_target_pairs={{0,8},{4,12},{8,0},{12,4},{1,9},{5,13},{9,1},{13,5},{2,10},{6,14},... | collective-permute-start | bytes 196616 | tf_op jit(solution)/shard_map/ppermute | solution.py:189
  13.9 3.9 %collective-permute-start.1 = (f32[8,4,256]{2,1,0:T(4,128)S(1)}, f32[8,4,256]{2,1,0:T(4,128)S(1)}, u32[]{:S(2)}, u32[]{:S(2)}) collective-permute-start(f32[8,4,256]{2,1,0:T(4,128)S(1)} %get-tuple-element.15), channel_id=1, source_target_pairs={{0,2},{2,0},{1,3},{3,1},{4,6},{6,4},{5,7},{7,5},{8,10},{10,8},{9,1... | collective-permute-start | bytes 98312 | tf_op jit(solution)/shard_map/ppermute | solution.py:153

commit v4 on v3

--- a/solution.py
+++ b/solution.py
@@ -63,7 +63,10 @@
         copy.wait()
 
 
-def moved(*pairs):
+BALANCE = 313
+
+
+def moved(beside, *pairs):
     return pl.pallas_call(
         move_kernel,
         out_shape=[space(x.shape, x.dtype) for x, space in pairs],
@@ -71,7 +74,7 @@
         out_specs=[pl.BlockSpec(memory_space=space) for _, space in pairs],
         scratch_shapes=[pltpu.SemaphoreType.DMA((len(pairs),))],
         compiler_params=pltpu.CompilerParams(vmem_limit_bytes=32 * MIB),
-        cost_estimate=COST,
+        cost_estimate=pl.CostEstimate(flops=BALANCE * beside.size * beside.dtype.itemsize, bytes_accessed=0, transcendentals=0),
     )(*[pltpu.with_memory_space_constraint(x, pltpu.HBM) for x, _ in pairs])
 
 
@@ -93,6 +96,9 @@
             out_ref[at + layer] = jnp.where(
                 here != groups - 1, now_ref[rows - WIDTH + layer], 0.0
             )
+        at += WIDTH
+    for rest in range(at, out_ref.shape[0]):
+        out_ref[rest] = jnp.zeros((depth, width), jnp.float32)
     if len(edge_refs) == 1:
         at_top = lax.axis_index("depth") == 0
         for row in range(rows):
@@ -107,7 +113,7 @@
 
 def source_of(image, offset_of, background, now, earlier, step, groups, half_span, edges):
     rows, depth, width = background.shape
-    extra = WIDTH * ((step == 1) + (step == groups - 1))
+    extra = WIDTH * ((step == 1) + (step == groups - 1)) + (edges > 0)
     return pl.pallas_call(
         functools.partial(source_kernel, half_span, step, groups),
         out_shape=[pltpu.VMEM((rows + extra, depth, width), jnp.float32)]
@@ -119,15 +125,12 @@
     )(offset_of, image, background, now, earlier)
 
 
-def step_kernel(half_span, offset_ref, image_ref, background_ref, now_ref, above_ref, below_ref, prev_ref, courant_ref, out_ref, deep_ref):
+def step_kernel(half_span, offset_ref, image_ref, background_ref, now_ref, prev_ref, courant_ref, out_ref, deep_ref):
     rows, depth, width = now_ref.shape
-    at = lax.axis_index("depth")
     deep_ref[:, 2 * WIDTH : 2 * WIDTH + depth] = now_ref[...]
-    deep_ref[:, WIDTH : 2 * WIDTH] = jnp.where(
-        at != 0, above_ref[...], 0.0
-    )
-    deep_ref[:, 2 * WIDTH + depth : 3 * WIDTH + depth] = jnp.where(
-        at != lax.axis_size("depth") - 1, below_ref[...], 0.0
+    deep_ref[:, WIDTH : 2 * WIDTH] = jnp.zeros((rows, WIDTH, width), jnp.float32)
+    deep_ref[:, 2 * WIDTH + depth : 3 * WIDTH + depth] = jnp.zeros(
+        (rows, WIDTH, width), jnp.float32
     )
     lane = lax.broadcasted_iota(jnp.int32, (depth, width), 1)
     own = slab_sums(half_span, offset_ref, image_ref, background_ref, lax.axis_index("off"))
@@ -147,6 +150,33 @@
         out_ref[row] = 2.0 * centre - prev_ref[row] + courant_ref[row] * (bending + own[row])
 
 
+def deep_kernel(base_ref, above_ref, below_ref, courant_ref, out_ref):
+    rows, depth, width = base_ref.shape
+    at = lax.axis_index("depth")
+    inside_above = (at != 0).astype(jnp.float32)
+    inside_below = (at != lax.axis_size("depth") - 1).astype(jnp.float32)
+    gap = jnp.zeros((depth - 2 * WIDTH, width), jnp.float32)
+    for row in range(rows):
+        above = above_ref[row] * inside_above
+        below = below_ref[row] * inside_below
+        upper, lower = [], []
+        for layer in range(WIDTH):
+            upper.append(
+                sum(
+                    STENCIL[radius] * above[WIDTH + layer - radius : WIDTH + layer - radius + 1]
+                    for radius in range(layer + 1, WIDTH + 1)
+                )
+            )
+            lower.append(
+                sum(
+                    STENCIL[radius] * below[layer + radius - WIDTH : layer + radius - WIDTH + 1]
+                    for radius in range(WIDTH - layer, WIDTH + 1)
+                )
+            )
+        bending = jnp.concatenate(upper + [gap] + lower, axis=0)
+        out_ref[row] = base_ref[row] + courant_ref[row] * bending
+
+
 def deep_layers(edges):
     count = lax.axis_size("depth")
     if count == 2:
@@ -168,8 +198,9 @@
         slabs[step] = lax.ppermute(
             own_slab, "off", [(i, (i + step) % groups) for i in range(groups)]
         )
-    held, now, cells, own_slab = moved(
-        (image, pltpu.VMEM),
+    held = pltpu.with_memory_space_constraint(image, pltpu.VMEM)
+    now, cells, own_slab = moved(
+        image,
         (wave_now[0], pltpu.VMEM),
         (offset_of, pltpu.SMEM),
         (own_slab, pltpu.VMEM),
@@ -191,15 +222,24 @@
 
     base = pl.pallas_call(
         functools.partial(step_kernel, half_span),
-        out_shape=jax.ShapeDtypeStruct(now.shape, jnp.float32),
-        in_specs=[SMEM] + [VMEM] * 7,
+        out_shape=pltpu.VMEM(now.shape, jnp.float32),
+        in_specs=[SMEM] + [VMEM] * 5,
         out_specs=VMEM,
         scratch_shapes=[pltpu.VMEM((rows, depth + 4 * WIDTH, width), jnp.float32)],
         compiler_params=pltpu.CompilerParams(vmem_limit_bytes=32 * MIB),
         cost_estimate=COST,
-    )(cells, held, own_slab, now, above, below, prev, courant)
-
-    after, before = returned[0][rows : rows + WIDTH], returned[-1][-WIDTH:]
+    )(cells, held, own_slab, now, prev, courant)
+    base = pl.pallas_call(
+        deep_kernel,
+        out_shape=pltpu.VMEM(now.shape, jnp.float32),
+        in_specs=[VMEM] * 4,
+        out_specs=VMEM,
+        compiler_params=pltpu.CompilerParams(vmem_limit_bytes=32 * MIB),
+        cost_estimate=COST,
+    )(base, above, below, courant)
+
+    at = rows if groups > 2 else rows + WIDTH
+    after, before = returned[0][rows : rows + WIDTH], returned[-1][at : at + WIDTH]
     beside = jnp.concatenate([before, jnp.zeros_like(now), after], axis=0)
     sums = functools.reduce(jnp.add, [part[:rows] for part in returned])
     for radius in range(1, WIDTH + 1):

time: 20.6 us -> 20 us (0.971)
  Pallas kernels: 4.41 us -> 3.18 us
  waiting for transfers between devices: 3.2 us -> 4.23 us
  starting transfers between devices: 11.9 us -> 11.5 us
    pallas_call x1, Pallas kernels: 2.23 us -> 0.94 us  [moved(): pl.pallas_call(move_kernel, out_shape=[space(x.shape, x.dtype) for x, spa...]
    ppermute x3, waiting for transfers between devices: 0.01 us -> 0.97 us  [on_device(): lax.ppermute(own_slab, 'off', [(i, (i + step) % groups) for i in range(gr...]
    ppermute x3, waiting for transfers between devices: 0.99 us -> 1.68 us  [on_device(): lax.ppermute(part.astype(jnp.float16), 'off', back).astype(jnp.float32)]
    ppermute x1, waiting for transfers between devices: 2.2 us -> 1.58 us  [deep_layers(): other = lax.ppermute(edges[0], 'depth', [(0, 1), (1, 0)])]
    ppermute x1, starting transfers between devices: 1.71 us -> 1.49 us  [deep_layers(): other = lax.ppermute(edges[0], 'depth', [(0, 1), (1, 0)])]
    pallas_call x1 -> x2, Pallas kernels: 0.85 us -> 0.91 us  [the longest x1 0.83 us: on_device(): pl.pallas_call(functools.partial(step_kernel, half_span), out_shape=pltpu...]
  transfers between devices with their start and end apart: 7 -> 7, of which waited for: 2 -> 5; matrix products, arithmetic and copies ran while one was open for 0% -> 0% of each run, Pallas kernels for 22% -> 16%
where the time goes in v4:
time: 20 us; the launch traced here: 19.9 us
  starting transfers between devices  11.5 us (58%)
  waiting for transfers between devices  4.23 us (21%)
  Pallas kernels  3.18 us (16%)
  other arithmetic  0.8 us (4%)
    ppermute x3, starting transfers between devices, on_device(): lax.ppermute(own_slab, 'off', [(i, (i + step) % groups) for i in range(gr...  6.06 us
    ppermute x3, starting transfers between devices, on_device(): lax.ppermute(part.astype(jnp.float16), 'off', back).astype(jnp.float32)  3.94 us
    ppermute x3, waiting for transfers between devices, on_device(): lax.ppermute(part.astype(jnp.float16), 'off', back).astype(jnp.float32)  1.68 us
    ppermute x1, waiting for transfers between devices, deep_layers(): other = lax.ppermute(edges[0], 'depth', [(0, 1), (1, 0)])  1.58 us
    ppermute x1, starting transfers between devices, deep_layers(): other = lax.ppermute(edges[0], 'depth', [(0, 1), (1, 0)])  1.49 us
    pallas_call x3, Pallas kernels, source_of(): pl.pallas_call(functools.partial(source_kernel, half_span, step, groups),...  1.32 us
    ppermute x3, waiting for transfers between devices, on_device(): lax.ppermute(own_slab, 'off', [(i, (i + step) % groups) for i in range(gr...  0.97 us
    pallas_call x1, Pallas kernels, moved(): pl.pallas_call(move_kernel, out_shape=[space(x.shape, x.dtype) for x, spa...  0.94 us
  transfers between devices with their start and end apart: 7, of which 5 were waited for; matrix products, arithmetic and copies ran while one was open for 0% of the time, Pallas kernels for 16%

profile of v4, /device:TPU:0, one launch (start us, length us, event | category | flops | bytes accessed | tf_op | source)
XLA Modules:
  0.0 19.9 jit_solution(3965523581566871181)
XLA Ops:
  0.0 3.0 %collective-permute-start = (bf16[8,16,256]{2,1,0:T(8,128)(2,1)}, bf16[8,16,256]{2,1,0:T(8,128)(2,1)S(1)}, u32[]{:S(2)}, u32[]{:S(2)}) collective-permute-start(bf16[8,16,256]{2,1,0:T(8,128)(2,1)} %bitcast.7), channel_id=1, source_target_pairs={{0,4},{4,8},{8,12},{12,0},{1,5},{5,9},{9,13},{13,1},{2,6},{6,10},{... | collective-permute-start | bytes 196616 | tf_op jit(solution)/shard_map/ppermute | solution.py:198
  3.0 2.1 %collective-permute-start.4 = (bf16[8,16,256]{2,1,0:T(8,128)(2,1)}, bf16[8,16,256]{2,1,0:T(8,128)(2,1)S(1)}, u32[]{:S(2)}, u32[]{:S(2)}) collective-permute-start(bf16[8,16,256]{2,1,0:T(8,128)(2,1)} %bitcast.8), channel_id=1, source_target_pairs={{0,12},{4,0},{8,4},{12,8},{1,13},{5,1},{9,5},{13,9},{2,14},{6,2},{... | collective-permute-start | bytes 196616 | tf_op jit(solution)/shard_map/ppermute | solution.py:198
  5.1 1.0 %collective-permute-start.3 = (bf16[8,16,256]{2,1,0:T(8,128)(2,1)}, bf16[8,16,256]{2,1,0:T(8,128)(2,1)S(1)}, u32[]{:S(2)}, u32[]{:S(2)}) collective-permute-start(bf16[8,16,256]{2,1,0:T(8,128)(2,1)} %bitcast.9), channel_id=1, source_target_pairs={{0,8},{4,12},{8,0},{12,4},{1,9},{5,13},{9,1},{13,5},{2,10},{6,14},... | collective-permute-start | bytes 196616 | tf_op jit(solution)/shard_map/ppermute | solution.py:198
  6.1 0.9 %shard_map.64 = (f32[8,16,256]{2,1,0:T(8,128)S(1)}, s32[16]{0:T(128)S(4)}, bf16[8,16,256]{2,1,0:T(8,128)(2,1)S(1)}) custom-call(f32[8,16,256]{2,1,0:T(8,128)} %bitcast.6, s32[16]{0:T(128)} %refs_1_.1, bf16[8,16,256]{2,1,0:T(8,128)(2,1)} %bitcast.10), custom_call_target="tpu_custom_call" | custom-call | flops 1312817152 | tf_op jit(solution)/shard_map/pallas_call | solution.py:70
  7.0 0.6 %collective-permute-done.background_ref = bf16[8,16,256]{2,1,0:T(8,128)(2,1)S(1)} collective-permute-done((bf16[8,16,256]{2,1,0:T(8,128)(2,1)}, bf16[8,16,256]{2,1,0:T(8,128)(2,1)S(1)}, u32[]{:S(2)}, u32[]{:S(2)}) %collective-permute-start) | collective-permute-done | bytes 65568 | tf_op jit(solution)/shard_map/ppermute | solution.py:198
  7.7 0.4 %shard_map.66 = (f32[13,16,256]{2,1,0:T(8,128)S(1)}, f32[8,4,256]{2,1,0:T(4,128)S(1)}) custom-call(s32[16]{0:T(128)S(4)} %get-tuple-element.10.offset_ref, bf16[16,32,16,256]{3,2,1,0:T(8,128)(2,1)S(1)} %copy-done, bf16[8,16,256]{2,1,0:T(8,128)(2,1)S(1)} %collective-permute-done.background_ref, f32[8,16,256]{2,1,0:T(8,128)S(1)} %get-tuple-element.12.now_ref.earlier_ref, ...), custom_call_target="tpu_custom_call" | custom-call | flops 1000 | bytes 1000 | tf_op jit(solution)/shard_map/pallas_call | solution.py:117
  8.1 0.0 copy-start.1
  8.2 0.0 copy-start.2
  8.2 1.9 %collective-permute-start.2 = (f16[13,16,256]{2,1,0:T(8,128)(2,1)S(1)}, f16[13,16,256]{2,1,0:T(8,128)(2,1)S(1)}, u32[]{:S(2)}, u32[]{:S(2)}) collective-permute-start(f16[13,16,256]{2,1,0:T(8,128)(2,1)S(1)} %convert_element_type.18), channel_id=1, source_target_pairs={{0,12},{4,0},{8,4},{12,8},{1,13},{5,1},{9,5},{13,9},{2,14},{6,2},{... | collective-permute-start | bytes 319496 | tf_op jit(solution)/shard_map/ppermute | solution.py:220
  10.1 0.0 collective-permute-done.4.background_ref
  10.1 0.4 %shard_map.68.earlier_ref = f32[12,16,256]{2,1,0:T(8,128)S(1)} custom-call(s32[16]{0:T(128)S(4)} %get-tuple-element.10.offset_ref, bf16[16,32,16,256]{3,2,1,0:T(8,128)(2,1)S(1)} %copy-done, bf16[8,16,256]{2,1,0:T(8,128)(2,1)S(1)} %collective-permute-done.4.background_ref, f32[8,16,256]{2,1,0:T(8,128)S(1)} %get-tuple-element.12.now_ref.earlier_ref, ...), custom_call_target="tpu_custom_call" | custom-call | flops 1000 | bytes 1000 | tf_op jit(solution)/shard_map/pallas_call | solution.py:117
  10.6 1.1 %collective-permute-start.6 = (f16[12,16,256]{2,1,0:T(8,128)(2,1)S(1)}, f16[12,16,256]{2,1,0:T(8,128)(2,1)S(1)}, u32[]{:S(2)}, u32[]{:S(2)}) collective-permute-start(f16[12,16,256]{2,1,0:T(8,128)(2,1)S(1)} %convert_element_type.22), channel_id=1, source_target_pairs={{0,4},{4,8},{8,12},{12,0},{1,5},{5,9},{9,13},{13,1},{2,6},{6,10},{... | collective-permute-start | bytes 294920 | tf_op jit(solution)/shard_map/ppermute | solution.py:220
  11.7 0.3 %collective-permute-done.3.background_ref = bf16[8,16,256]{2,1,0:T(8,128)(2,1)S(1)} collective-permute-done((bf16[8,16,256]{2,1,0:T(8,128)(2,1)}, bf16[8,16,256]{2,1,0:T(8,128)(2,1)S(1)}, u32[]{:S(2)}, u32[]{:S(2)}) %collective-permute-start.3) | collective-permute-done | bytes 65568 | tf_op jit(solution)/shard_map/ppermute | solution.py:198
  12.0 0.4 %shard_map.69 = f32[8,16,256]{2,1,0:T(8,128)S(1)} custom-call(s32[16]{0:T(128)S(4)} %get-tuple-element.10.offset_ref, bf16[16,32,16,256]{3,2,1,0:T(8,128)(2,1)S(1)} %copy-done, bf16[8,16,256]{2,1,0:T(8,128)(2,1)S(1)} %collective-permute-done.3.background_ref, f32[8,16,256]{2,1,0:T(8,128)S(1)} %get-tuple-element.12.now_ref.earlier_ref, ...), custom_call_target="tpu_custom_call" | custom-call | flops 1000 | bytes 1000 | tf_op jit(solution)/shard_map/pallas_call | solution.py:117
  12.5 0.9 %collective-permute-start.5 = (f16[8,16,256]{2,1,0:T(8,128)(2,1)S(1)}, f16[8,16,256]{2,1,0:T(8,128)(2,1)S(1)}, u32[]{:S(2)}, u32[]{:S(2)}) collective-permute-start(f16[8,16,256]{2,1,0:T(8,128)(2,1)S(1)} %convert_element_type.20), channel_id=1, source_target_pairs={{0,8},{4,12},{8,0},{12,4},{1,9},{5,13},{9,1},{13,5},{2,10},{6,14},... | collective-permute-start | bytes 196616 | tf_op jit(solution)/shard_map/ppermute | solution.py:220
  13.4 1.5 %collective-permute-start.1 = (f32[8,4,256]{2,1,0:T(4,128)S(1)}, f32[8,4,256]{2,1,0:T(4,128)S(1)}, u32[]{:S(2)}, u32[]{:S(2)}) collective-permute-start(f32[8,4,256]{2,1,0:T(4,128)S(1)} %get-tuple-element.13), channel_id=1, source_target_pairs={{0,2},{2,0},{1,3},{3,1},{4,6},{6,4},{5,7},{7,5},{8,10},{10,8},{9,1... | collective-permute-start | bytes 98312 | tf_op jit(solution)/shard_map/ppermute | solution.py:183
  14.9 0.0 copy-done.1
  14.9 0.8 %shard_map.65.base_ref = f32[8,16,256]{2,1,0:T(8,128)S(1)} custom-call(s32[16]{0:T(128)S(4)} %get-tuple-element.10.offset_ref, bf16[16,32,16,256]{3,2,1,0:T(8,128)(2,1)S(1)} %copy-done, bf16[8,16,256]{2,1,0:T(8,128)(2,1)S(1)} %get-tuple-element.11.background_ref, f32[8,16,256]{2,1,0:T(8,128)S(1)} %get-tuple-element.12.now_ref.earlier_ref, ...), custom_call_target="tpu_custom_call" | custom-call | flops 1000 | bytes 1000 | tf_op jit(solution)/shard_map/pallas_call | solution.py:223
  15.7 1.6 %collective-permute-done.1.above_ref.below_ref = f32[8,4,256]{2,1,0:T(4,128)S(1)} collective-permute-done((f32[8,4,256]{2,1,0:T(4,128)S(1)}, f32[8,4,256]{2,1,0:T(4,128)S(1)}, u32[]{:S(2)}, u32[]{:S(2)}) %collective-permute-start.1) | collective-permute-done | bytes 32800 | tf_op jit(solution)/shard_map/ppermute | solution.py:183
  17.3 0.1 shard_map.67
  17.4 0.4 %collective-permute-done.6 = f16[12,16,256]{2,1,0:T(8,128)(2,1)S(1)} collective-permute-done((f16[12,16,256]{2,1,0:T(8,128)(2,1)S(1)}, f16[12,16,256]{2,1,0:T(8,128)(2,1)S(1)}, u32[]{:S(2)}, u32[]{:S(2)}) %collective-permute-start.6) | collective-permute-done | bytes 98336 | tf_op jit(solution)/shard_map/ppermute | solution.py:220
  17.8 0.0 collective-permute-done.2
  17.9 1.2 %collective-permute-done.5 = f16[8,16,256]{2,1,0:T(8,128)(2,1)S(1)} collective-permute-done((f16[8,16,256]{2,1,0:T(8,128)(2,1)S(1)}, f16[8,16,256]{2,1,0:T(8,128)(2,1)S(1)}, u32[]{:S(2)}, u32[]{:S(2)}) %collective-permute-start.5) | collective-permute-done | bytes 65568 | tf_op jit(solution)/shard_map/ppermute | solution.py:220
  19.1 0.7 %fusion.8 = f32[1,8,16,256]{3,2,1,0:T(8,128)} fusion(f32[8,16,256]{2,1,0:T(8,128)S(1)} %shard_map.67, f32[8,16,256]{2,1,0:T(8,128)S(1)} %copy-done.1, f32[4,16,256]{2,1,0:T(8,128)S(1)} %slice.58, f32[4,16,256]{2,1,0:T(8,128)S(1)} %slice.59, f32[12,16,256]{2,1,0:T(8,128)S(1)} %convert_element_type.23, f32[13,16,256]{2,1,0:T(8,128)S(1)} %convert_element_type.19, ...), kind=kLoop, calls=%fused_computation.16 | loop fusion | flops 557056 | bytes 851968 | tf_op jit(solution)/shard_map/broadcast_in_dim | solution.py:250
  (10 shorter events, 0.1 us)
Async XLA Ops:
  0.0 7.7 %copy-start = (bf16[16,32,16,256]{3,2,1,0:T(8,128)(2,1)S(1)}, bf16[16,32,16,256]{3,2,1,0:T(8,128)(2,1)}, u32[]{:S(2)}) copy-start(bf16[16,32,16,256]{3,2,1,0:T(8,128)(2,1)} %image_ref.7) | copy-start | bytes 12582916
  0.0 7.7 %collective-permute-start = (bf16[8,16,256]{2,1,0:T(8,128)(2,1)}, bf16[8,16,256]{2,1,0:T(8,128)(2,1)S(1)}, u32[]{:S(2)}, u32[]{:S(2)}) collective-permute-start(bf16[8,16,256]{2,1,0:T(8,128)(2,1)} %bitcast.7), channel_id=1, source_target_pairs={{0,4},{4,8},{8,12},{12,0},{1,5},{5,9},{9,13},{13,1},{2,6},{6,10},{... | collective-permute-start | bytes 196616 | tf_op jit(solution)/shard_map/ppermute | solution.py:198
  3.0 7.1 %collective-permute-start.4 = (bf16[8,16,256]{2,1,0:T(8,128)(2,1)}, bf16[8,16,256]{2,1,0:T(8,128)(2,1)S(1)}, u32[]{:S(2)}, u32[]{:S(2)}) collective-permute-start(bf16[8,16,256]{2,1,0:T(8,128)(2,1)} %bitcast.8), channel_id=1, source_target_pairs={{0,12},{4,0},{8,4},{12,8},{1,13},{5,1},{9,5},{13,9},{2,14},{6,2},{... | collective-permute-start | bytes 196616 | tf_op jit(solution)/shard_map/ppermute | solution.py:198
  5.1 6.9 %collective-permute-start.3 = (bf16[8,16,256]{2,1,0:T(8,128)(2,1)}, bf16[8,16,256]{2,1,0:T(8,128)(2,1)S(1)}, u32[]{:S(2)}, u32[]{:S(2)}) collective-permute-start(bf16[8,16,256]{2,1,0:T(8,128)(2,1)} %bitcast.9), channel_id=1, source_target_pairs={{0,8},{4,12},{8,0},{12,4},{1,9},{5,13},{9,1},{13,5},{2,10},{6,14},... | collective-permute-start | bytes 196616 | tf_op jit(solution)/shard_map/ppermute | solution.py:198
  8.1 6.7 %copy-start.1 = (f32[8,16,256]{2,1,0:T(8,128)S(1)}, f32[8,16,256]{2,1,0:T(8,128)}, u32[]{:S(2)}) copy-start(f32[8,16,256]{2,1,0:T(8,128)} %courant_ref.3) | copy-start | bytes 393220
  8.2 6.7 %copy-start.2 = (f32[1,8,16,256]{3,2,1,0:T(8,128)S(1)}, f32[1,8,16,256]{3,2,1,0:T(8,128)}, u32[]{:S(2)}) copy-start(f32[1,8,16,256]{3,2,1,0:T(8,128)} %param.10) | copy-start | bytes 393220
  8.2 9.7 %collective-permute-start.2 = (f16[13,16,256]{2,1,0:T(8,128)(2,1)S(1)}, f16[13,16,256]{2,1,0:T(8,128)(2,1)S(1)}, u32[]{:S(2)}, u32[]{:S(2)}) collective-permute-start(f16[13,16,256]{2,1,0:T(8,128)(2,1)S(1)} %convert_element_type.18), channel_id=1, source_target_pairs={{0,12},{4,0},{8,4},{12,8},{1,13},{5,1},{9,5},{13,9},{2,14},{6,2},{... | collective-permute-start | bytes 319496 | tf_op jit(solution)/shard_map/ppermute | solution.py:220
  10.6 7.2 %collective-permute-start.6 = (f16[12,16,256]{2,1,0:T(8,128)(2,1)S(1)}, f16[12,16,256]{2,1,0:T(8,128)(2,1)S(1)}, u32[]{:S(2)}, u32[]{:S(2)}) collective-permute-start(f16[12,16,256]{2,1,0:T(8,128)(2,1)S(1)} %convert_element_type.22), channel_id=1, source_target_pairs={{0,4},{4,8},{8,12},{12,0},{1,5},{5,9},{9,13},{13,1},{2,6},{6,10},{... | collective-permute-start | bytes 294920 | tf_op jit(solution)/shard_map/ppermute | solution.py:220
  12.5 6.7 %collective-permute-start.5 = (f16[8,16,256]{2,1,0:T(8,128)(2,1)S(1)}, f16[8,16,256]{2,1,0:T(8,128)(2,1)S(1)}, u32[]{:S(2)}, u32[]{:S(2)}) collective-permute-start(f16[8,16,256]{2,1,0:T(8,128)(2,1)S(1)} %convert_element_type.20), channel_id=1, source_target_pairs={{0,8},{4,12},{8,0},{12,4},{1,9},{5,13},{9,1},{13,5},{2,10},{6,14},... | collective-permute-start | bytes 196616 | tf_op jit(solution)/shard_map/ppermute | solution.py:220
  13.4 3.9 %collective-permute-start.1 = (f32[8,4,256]{2,1,0:T(4,128)S(1)}, f32[8,4,256]{2,1,0:T(4,128)S(1)}, u32[]{:S(2)}, u32[]{:S(2)}) collective-permute-start(f32[8,4,256]{2,1,0:T(4,128)S(1)} %get-tuple-element.13), channel_id=1, source_target_pairs={{0,2},{2,0},{1,3},{3,1},{4,6},{6,4},{5,7},{7,5},{8,10},{10,8},{9,1... | collective-permute-start | bytes 98312 | tf_op jit(solution)/shard_map/ppermute | solution.py:183

commit v5 on v4

--- a/solution.py
+++ b/solution.py
@@ -63,7 +63,7 @@
         copy.wait()
 
 
-BALANCE = 313
+SCALE = 64.0
 
 
 def moved(beside, *pairs):
@@ -74,7 +74,7 @@
         out_specs=[pl.BlockSpec(memory_space=space) for _, space in pairs],
         scratch_shapes=[pltpu.SemaphoreType.DMA((len(pairs),))],
         compiler_params=pltpu.CompilerParams(vmem_limit_bytes=32 * MIB),
-        cost_estimate=pl.CostEstimate(flops=BALANCE * beside.size * beside.dtype.itemsize, bytes_accessed=0, transcendentals=0),
+        cost_estimate=pl.CostEstimate(flops=0, bytes_accessed=0, transcendentals=5 * beside.size // 3),
     )(*[pltpu.with_memory_space_constraint(x, pltpu.HBM) for x, _ in pairs])
 
 
@@ -85,20 +85,17 @@
     slab = lax.rem(here - step + groups, groups)
     totals = slab_sums(half_span, offset_ref, image_ref, background_ref, slab)
     for row in range(rows):
-        out_ref[row] = totals[row]
+        out_ref[row] = SCALE * totals[row]
     at = rows
     if step == 1:
         for layer in range(WIDTH):
-            out_ref[at + layer] = jnp.where(here != 0, now_ref[layer], 0.0)
+            out_ref[at + layer] = jnp.where(here != 0, SCALE * now_ref[layer], 0.0)
         at += WIDTH
     if step == groups - 1:
         for layer in range(WIDTH):
             out_ref[at + layer] = jnp.where(
-                here != groups - 1, now_ref[rows - WIDTH + layer], 0.0
-            )
-        at += WIDTH
-    for rest in range(at, out_ref.shape[0]):
-        out_ref[rest] = jnp.zeros((depth, width), jnp.float32)
+                here != groups - 1, SCALE * now_ref[rows - WIDTH + layer], 0.0
+            )
     if len(edge_refs) == 1:
         at_top = lax.axis_index("depth") == 0
         for row in range(rows):
@@ -113,7 +110,7 @@
 
 def source_of(image, offset_of, background, now, earlier, step, groups, half_span, edges):
     rows, depth, width = background.shape
-    extra = WIDTH * ((step == 1) + (step == groups - 1)) + (edges > 0)
+    extra = WIDTH * ((step == 1) + (step == groups - 1))
     return pl.pallas_call(
         functools.partial(source_kernel, half_span, step, groups),
         out_shape=[pltpu.VMEM((rows + extra, depth, width), jnp.float32)]
@@ -241,13 +238,13 @@
     at = rows if groups > 2 else rows + WIDTH
     after, before = returned[0][rows : rows + WIDTH], returned[-1][at : at + WIDTH]
     beside = jnp.concatenate([before, jnp.zeros_like(now), after], axis=0)
-    sums = functools.reduce(jnp.add, [part[:rows] for part in returned])
+    sums = functools.reduce(jnp.add, [part[:rows] for part in reversed(returned)])
     for radius in range(1, WIDTH + 1):
         sums = sums + STENCIL[radius] * (
             beside[WIDTH - radius : WIDTH - radius + rows]
             + beside[WIDTH + radius : WIDTH + radius + rows]
         )
-    return (base + courant * sums)[None]
+    return (base + courant * (sums * (1.0 / SCALE)))[None]
 
 
 def solution(mesh):

time: 20 us -> 19.9 us (level)
  waiting for transfers between devices: 4.23 us -> 3.61 us
  starting transfers between devices: 11.5 us -> 12 us
    ppermute x3, starting transfers between devices: 3.94 us -> 4.62 us  [on_device(): lax.ppermute(part.astype(jnp.float16), 'off', back).astype(jnp.float32)]
    ppermute x3, waiting for transfers between devices: 1.68 us -> 1.17 us  [on_device(): lax.ppermute(part.astype(jnp.float16), 'off', back).astype(jnp.float32)]
    ppermute x3, waiting for transfers between devices: 0.97 us -> 0.73 us  [on_device(): lax.ppermute(own_slab, 'off', [(i, (i + step) % groups) for i in range(gr...]
  transfers between devices with their start and end apart: 7 -> 7, of which waited for: 5 -> 4; matrix products, arithmetic and copies ran while one was open for 0% -> 0% of each run, Pallas kernels for 16% -> 16%
where the time goes in v5:
time: 19.9 us; the launch traced here: 19.8 us
  starting transfers between devices  12 us (60%)
  waiting for transfers between devices  3.61 us (18%)
  Pallas kernels  3.19 us (16%)
  other arithmetic  0.8 us (4%)
    ppermute x3, starting transfers between devices, on_device(): lax.ppermute(own_slab, 'off', [(i, (i + step) % groups) for i in range(gr...  6.06 us
    ppermute x3, starting transfers between devices, on_device(): lax.ppermute(part.astype(jnp.float16), 'off', back).astype(jnp.float32)  4.62 us
    ppermute x1, waiting for transfers between devices, deep_layers(): other = lax.ppermute(edges[0], 'depth', [(0, 1), (1, 0)])  1.71 us
    ppermute x1, starting transfers between devices, deep_layers(): other = lax.ppermute(edges[0], 'depth', [(0, 1), (1, 0)])  1.36 us
    pallas_call x3, Pallas kernels, source_of(): pl.pallas_call(functools.partial(source_kernel, half_span, step, groups),...  1.34 us
    ppermute x3, waiting for transfers between devices, on_device(): lax.ppermute(part.astype(jnp.float16), 'off', back).astype(jnp.float32)  1.17 us
    pallas_call x1, Pallas kernels, moved(): pl.pallas_call(move_kernel, out_shape=[space(x.shape, x.dtype) for x, spa...  0.94 us
    pallas_call x1, Pallas kernels, on_device(): pl.pallas_call(functools.partial(step_kernel, half_span), out_shape=pltpu...  0.83 us
  transfers between devices with their start and end apart: 7, of which 4 were waited for; matrix products, arithmetic and copies ran while one was open for 0% of the time, Pallas kernels for 16%

profile of v5, /device:TPU:0, one launch (start us, length us, event | category | flops | bytes accessed | tf_op | source)
XLA Modules:
  0.0 19.8 jit_solution(14714688343154531594)
XLA Ops:
  0.0 3.0 %collective-permute-start = (bf16[8,16,256]{2,1,0:T(8,128)(2,1)}, bf16[8,16,256]{2,1,0:T(8,128)(2,1)S(1)}, u32[]{:S(2)}, u32[]{:S(2)}) collective-permute-start(bf16[8,16,256]{2,1,0:T(8,128)(2,1)} %bitcast.7), channel_id=1, source_target_pairs={{0,4},{4,8},{8,12},{12,0},{1,5},{5,9},{9,13},{13,1},{2,6},{6,10},{... | collective-permute-start | bytes 196616 | tf_op jit(solution)/shard_map/ppermute | solution.py:195
  3.0 2.1 %collective-permute-start.2 = (bf16[8,16,256]{2,1,0:T(8,128)(2,1)}, bf16[8,16,256]{2,1,0:T(8,128)(2,1)S(1)}, u32[]{:S(2)}, u32[]{:S(2)}) collective-permute-start(bf16[8,16,256]{2,1,0:T(8,128)(2,1)} %bitcast.8), channel_id=1, source_target_pairs={{0,12},{4,0},{8,4},{12,8},{1,13},{5,1},{9,5},{13,9},{2,14},{6,2},{... | collective-permute-start | bytes 196616 | tf_op jit(solution)/shard_map/ppermute | solution.py:195
  5.1 1.0 %collective-permute-start.4 = (bf16[8,16,256]{2,1,0:T(8,128)(2,1)}, bf16[8,16,256]{2,1,0:T(8,128)(2,1)S(1)}, u32[]{:S(2)}, u32[]{:S(2)}) collective-permute-start(bf16[8,16,256]{2,1,0:T(8,128)(2,1)} %bitcast.9), channel_id=1, source_target_pairs={{0,8},{4,12},{8,0},{12,4},{1,9},{5,13},{9,1},{13,5},{2,10},{6,14},... | collective-permute-start | bytes 196616 | tf_op jit(solution)/shard_map/ppermute | solution.py:195
  6.1 0.9 %shard_map.64 = (f32[8,16,256]{2,1,0:T(8,128)S(1)}, s32[16]{0:T(128)S(4)}, bf16[8,16,256]{2,1,0:T(8,128)(2,1)S(1)}) custom-call(f32[8,16,256]{2,1,0:T(8,128)} %bitcast.6, s32[16]{0:T(128)} %refs_1_.1, bf16[8,16,256]{2,1,0:T(8,128)(2,1)} %bitcast.10), custom_call_target="tpu_custom_call" | custom-call | tf_op jit(solution)/shard_map/pallas_call | solution.py:70
  7.0 0.6 %collective-permute-done.background_ref = bf16[8,16,256]{2,1,0:T(8,128)(2,1)S(1)} collective-permute-done((bf16[8,16,256]{2,1,0:T(8,128)(2,1)}, bf16[8,16,256]{2,1,0:T(8,128)(2,1)S(1)}, u32[]{:S(2)}, u32[]{:S(2)}) %collective-permute-start) | collective-permute-done | bytes 65568 | tf_op jit(solution)/shard_map/ppermute | solution.py:195
  7.7 0.0 copy-done
  7.7 0.5 %shard_map.66 = (f32[12,16,256]{2,1,0:T(8,128)S(1)}, f32[8,4,256]{2,1,0:T(4,128)S(1)}) custom-call(s32[16]{0:T(128)S(4)} %get-tuple-element.10.offset_ref, bf16[16,32,16,256]{3,2,1,0:T(8,128)(2,1)S(1)} %copy-done, bf16[8,16,256]{2,1,0:T(8,128)(2,1)S(1)} %collective-permute-done.background_ref, f32[8,16,256]{2,1,0:T(8,128)S(1)} %get-tuple-element.12.now_ref.earlier_ref, ...), custom_call_target="tpu_custom_call" | custom-call | flops 1000 | bytes 1000 | tf_op jit(solution)/shard_map/pallas_call | solution.py:114
  8.1 0.1 collective-permute-done.2.background_ref
  8.2 0.4 %shard_map.68.earlier_ref = f32[12,16,256]{2,1,0:T(8,128)S(1)} custom-call(s32[16]{0:T(128)S(4)} %get-tuple-element.10.offset_ref, bf16[16,32,16,256]{3,2,1,0:T(8,128)(2,1)S(1)} %copy-done, bf16[8,16,256]{2,1,0:T(8,128)(2,1)S(1)} %collective-permute-done.2.background_ref, f32[8,16,256]{2,1,0:T(8,128)S(1)} %get-tuple-element.12.now_ref.earlier_ref, ...), custom_call_target="tpu_custom_call" | custom-call | flops 1000 | bytes 1000 | tf_op jit(solution)/shard_map/pallas_call | solution.py:114
  8.7 3.0 %collective-permute-start.3 = (f16[12,16,256]{2,1,0:T(8,128)(2,1)S(1)}, f16[12,16,256]{2,1,0:T(8,128)(2,1)S(1)}, u32[]{:S(2)}, u32[]{:S(2)}) collective-permute-start(f16[12,16,256]{2,1,0:T(8,128)(2,1)S(1)} %convert_element_type.18), channel_id=1, source_target_pairs={{0,4},{4,8},{8,12},{12,0},{1,5},{5,9},{9,13},{13,1},{2,6},{6,10},{... | collective-permute-start | bytes 294920 | tf_op jit(solution)/shard_map/ppermute | solution.py:217
  11.7 0.9 %collective-permute-start.6 = (f16[12,16,256]{2,1,0:T(8,128)(2,1)S(1)}, f16[12,16,256]{2,1,0:T(8,128)(2,1)S(1)}, u32[]{:S(2)}, u32[]{:S(2)}) collective-permute-start(f16[12,16,256]{2,1,0:T(8,128)(2,1)S(1)} %convert_element_type.22), channel_id=1, source_target_pairs={{0,12},{4,0},{8,4},{12,8},{1,13},{5,1},{9,5},{13,9},{2,14},{6,2},{... | collective-permute-start | bytes 294920 | tf_op jit(solution)/shard_map/ppermute | solution.py:217
  12.6 0.0 collective-permute-done.4.background_ref
  12.6 0.4 %shard_map.69 = f32[8,16,256]{2,1,0:T(8,128)S(1)} custom-call(s32[16]{0:T(128)S(4)} %get-tuple-element.10.offset_ref, bf16[16,32,16,256]{3,2,1,0:T(8,128)(2,1)S(1)} %copy-done, bf16[8,16,256]{2,1,0:T(8,128)(2,1)S(1)} %collective-permute-done.4.background_ref, f32[8,16,256]{2,1,0:T(8,128)S(1)} %get-tuple-element.12.now_ref.earlier_ref, ...), custom_call_target="tpu_custom_call" | custom-call | flops 1000 | bytes 1000 | tf_op jit(solution)/shard_map/pallas_call | solution.py:114
  13.1 0.7 %collective-permute-start.5 = (f16[8,16,256]{2,1,0:T(8,128)(2,1)S(1)}, f16[8,16,256]{2,1,0:T(8,128)(2,1)S(1)}, u32[]{:S(2)}, u32[]{:S(2)}) collective-permute-start(f16[8,16,256]{2,1,0:T(8,128)(2,1)S(1)} %convert_element_type.20), channel_id=1, source_target_pairs={{0,8},{4,12},{8,0},{12,4},{1,9},{5,13},{9,1},{13,5},{2,10},{6,14},... | collective-permute-start | bytes 196616 | tf_op jit(solution)/shard_map/ppermute | solution.py:217
  13.8 1.4 %collective-permute-start.1 = (f32[8,4,256]{2,1,0:T(4,128)S(1)}, f32[8,4,256]{2,1,0:T(4,128)S(1)}, u32[]{:S(2)}, u32[]{:S(2)}) collective-permute-start(f32[8,4,256]{2,1,0:T(4,128)S(1)} %get-tuple-element.13), channel_id=1, source_target_pairs={{0,2},{2,0},{1,3},{3,1},{4,6},{6,4},{5,7},{7,5},{8,10},{10,8},{9,1... | collective-permute-start | bytes 98312 | tf_op jit(solution)/shard_map/ppermute | solution.py:180
  15.2 0.0 copy-done.1
  15.2 0.0 copy-done.2
  15.2 0.8 %shard_map.65.base_ref = f32[8,16,256]{2,1,0:T(8,128)S(1)} custom-call(s32[16]{0:T(128)S(4)} %get-tuple-element.10.offset_ref, bf16[16,32,16,256]{3,2,1,0:T(8,128)(2,1)S(1)} %copy-done, bf16[8,16,256]{2,1,0:T(8,128)(2,1)S(1)} %get-tuple-element.11.background_ref, f32[8,16,256]{2,1,0:T(8,128)S(1)} %get-tuple-element.12.now_ref.earlier_ref, ...), custom_call_target="tpu_custom_call" | custom-call | flops 1000 | bytes 1000 | tf_op jit(solution)/shard_map/pallas_call | solution.py:220
  16.0 1.7 %collective-permute-done.1.above_ref.below_ref = f32[8,4,256]{2,1,0:T(4,128)S(1)} collective-permute-done((f32[8,4,256]{2,1,0:T(4,128)S(1)}, f32[8,4,256]{2,1,0:T(4,128)S(1)}, u32[]{:S(2)}, u32[]{:S(2)}) %collective-permute-start.1) | collective-permute-done | bytes 32800 | tf_op jit(solution)/shard_map/ppermute | solution.py:180
  17.7 0.1 shard_map.67
  17.8 0.0 collective-permute-done.3
  17.9 0.0 collective-permute-done.6
  17.9 1.2 %collective-permute-done.5 = f16[8,16,256]{2,1,0:T(8,128)(2,1)S(1)} collective-permute-done((f16[8,16,256]{2,1,0:T(8,128)(2,1)S(1)}, f16[8,16,256]{2,1,0:T(8,128)(2,1)S(1)}, u32[]{:S(2)}, u32[]{:S(2)}) %collective-permute-start.5) | collective-permute-done | bytes 65568 | tf_op jit(solution)/shard_map/ppermute | solution.py:217
  19.1 0.7 %fusion.9 = f32[1,8,16,256]{3,2,1,0:T(8,128)} fusion(f32[8,16,256]{2,1,0:T(8,128)S(1)} %shard_map.67, f32[8,16,256]{2,1,0:T(8,128)S(1)} %copy-done.1, f32[4,16,256]{2,1,0:T(8,128)S(1)} %slice.58, f32[4,16,256]{2,1,0:T(8,128)S(1)} %slice.59, f32[12,16,256]{2,1,0:T(8,128)S(1)} %convert_element_type.23, f32[12,16,256]{2,1,0:T(8,128)S(1)} %convert_element_type.19, ...), kind=kLoop, calls=%fused_computation.17 | loop fusion | flops 589824 | bytes 851968 | tf_op jit(solution)/shard_map/broadcast_in_dim | solution.py:247
  (10 shorter events, 0.1 us)
Async XLA Ops:
  0.0 7.7 %copy-start = (bf16[16,32,16,256]{3,2,1,0:T(8,128)(2,1)S(1)}, bf16[16,32,16,256]{3,2,1,0:T(8,128)(2,1)}, u32[]{:S(2)}) copy-start(bf16[16,32,16,256]{3,2,1,0:T(8,128)(2,1)} %image_ref.7) | copy-start | bytes 12582916
  0.0 7.7 %collective-permute-start = (bf16[8,16,256]{2,1,0:T(8,128)(2,1)}, bf16[8,16,256]{2,1,0:T(8,128)(2,1)S(1)}, u32[]{:S(2)}, u32[]{:S(2)}) collective-permute-start(bf16[8,16,256]{2,1,0:T(8,128)(2,1)} %bitcast.7), channel_id=1, source_target_pairs={{0,4},{4,8},{8,12},{12,0},{1,5},{5,9},{9,13},{13,1},{2,6},{6,10},{... | collective-permute-start | bytes 196616 | tf_op jit(solution)/shard_map/ppermute | solution.py:195
  3.0 5.2 %collective-permute-start.2 = (bf16[8,16,256]{2,1,0:T(8,128)(2,1)}, bf16[8,16,256]{2,1,0:T(8,128)(2,1)S(1)}, u32[]{:S(2)}, u32[]{:S(2)}) collective-permute-start(bf16[8,16,256]{2,1,0:T(8,128)(2,1)} %bitcast.8), channel_id=1, source_target_pairs={{0,12},{4,0},{8,4},{12,8},{1,13},{5,1},{9,5},{13,9},{2,14},{6,2},{... | collective-permute-start | bytes 196616 | tf_op jit(solution)/shard_map/ppermute | solution.py:195
  5.1 7.5 %collective-permute-start.4 = (bf16[8,16,256]{2,1,0:T(8,128)(2,1)}, bf16[8,16,256]{2,1,0:T(8,128)(2,1)S(1)}, u32[]{:S(2)}, u32[]{:S(2)}) collective-permute-start(bf16[8,16,256]{2,1,0:T(8,128)(2,1)} %bitcast.9), channel_id=1, source_target_pairs={{0,8},{4,12},{8,0},{12,4},{1,9},{5,13},{9,1},{13,5},{2,10},{6,14},... | collective-permute-start | bytes 196616 | tf_op jit(solution)/shard_map/ppermute | solution.py:195
  8.2 7.0 %copy-start.1 = (f32[8,16,256]{2,1,0:T(8,128)S(1)}, f32[8,16,256]{2,1,0:T(8,128)}, u32[]{:S(2)}) copy-start(f32[8,16,256]{2,1,0:T(8,128)} %courant_ref.3) | copy-start | bytes 393220
  8.2 7.0 %copy-start.2 = (f32[1,8,16,256]{3,2,1,0:T(8,128)S(1)}, f32[1,8,16,256]{3,2,1,0:T(8,128)}, u32[]{:S(2)}) copy-start(f32[1,8,16,256]{3,2,1,0:T(8,128)} %param.10) | copy-start | bytes 393220
  8.7 9.1 %collective-permute-start.3 = (f16[12,16,256]{2,1,0:T(8,128)(2,1)S(1)}, f16[12,16,256]{2,1,0:T(8,128)(2,1)S(1)}, u32[]{:S(2)}, u32[]{:S(2)}) collective-permute-start(f16[12,16,256]{2,1,0:T(8,128)(2,1)S(1)} %convert_element_type.18), channel_id=1, source_target_pairs={{0,4},{4,8},{8,12},{12,0},{1,5},{5,9},{9,13},{13,1},{2,6},{6,10},{... | collective-permute-start | bytes 294920 | tf_op jit(solution)/shard_map/ppermute | solution.py:217
  11.7 6.1 %collective-permute-start.6 = (f16[12,16,256]{2,1,0:T(8,128)(2,1)S(1)}, f16[12,16,256]{2,1,0:T(8,128)(2,1)S(1)}, u32[]{:S(2)}, u32[]{:S(2)}) collective-permute-start(f16[12,16,256]{2,1,0:T(8,128)(2,1)S(1)} %convert_element_type.22), channel_id=1, source_target_pairs={{0,12},{4,0},{8,4},{12,8},{1,13},{5,1},{9,5},{13,9},{2,14},{6,2},{... | collective-permute-start | bytes 294920 | tf_op jit(solution)/shard_map/ppermute | solution.py:217
  13.1 6.0 %collective-permute-start.5 = (f16[8,16,256]{2,1,0:T(8,128)(2,1)S(1)}, f16[8,16,256]{2,1,0:T(8,128)(2,1)S(1)}, u32[]{:S(2)}, u32[]{:S(2)}) collective-permute-start(f16[8,16,256]{2,1,0:T(8,128)(2,1)S(1)} %convert_element_type.20), channel_id=1, source_target_pairs={{0,8},{4,12},{8,0},{12,4},{1,9},{5,13},{9,1},{13,5},{2,10},{6,14},... | collective-permute-start | bytes 196616 | tf_op jit(solution)/shard_map/ppermute | solution.py:217
  13.8 3.9 %collective-permute-start.1 = (f32[8,4,256]{2,1,0:T(4,128)S(1)}, f32[8,4,256]{2,1,0:T(4,128)S(1)}, u32[]{:S(2)}, u32[]{:S(2)}) collective-permute-start(f32[8,4,256]{2,1,0:T(4,128)S(1)} %get-tuple-element.13), channel_id=1, source_target_pairs={{0,2},{2,0},{1,3},{3,1},{4,6},{6,4},{5,7},{7,5},{8,10},{10,8},{9,1... | collective-permute-start | bytes 98312 | tf_op jit(solution)/shard_map/ppermute | solution.py:180

commit v6 on v5

--- a/solution.py
+++ b/solution.py
@@ -237,8 +237,9 @@
 
     at = rows if groups > 2 else rows + WIDTH
     after, before = returned[0][rows : rows + WIDTH], returned[-1][at : at + WIDTH]
-    beside = jnp.concatenate([before, jnp.zeros_like(now), after], axis=0)
-    sums = functools.reduce(jnp.add, [part[:rows] for part in reversed(returned)])
+    beside = jnp.pad(before, ((0, WIDTH + rows), (0, 0), (0, 0)))
+    beside = beside + jnp.pad(after, ((WIDTH + rows, 0), (0, 0), (0, 0)))
+    sums = functools.reduce(jnp.add, [returned[at][:rows] for at in range(-1, groups - 2)])
     for radius in range(1, WIDTH + 1):
         sums = sums + STENCIL[radius] * (
             beside[WIDTH - radius : WIDTH - radius + rows]

time: 19.9 us -> 19.9 us (level)
  no operation moved by 1% of the time
where the time goes in v6:
time: 19.9 us; the launch traced here: 19.8 us
  starting transfers between devices  12 us (60%)
  waiting for transfers between devices  3.61 us (18%)
  Pallas kernels  3.19 us (16%)
  other arithmetic  0.8 us (4%)
    ppermute x3, starting transfers between devices, on_device(): lax.ppermute(own_slab, 'off', [(i, (i + step) % groups) for i in range(gr...  6.06 us
    ppermute x3, starting transfers between devices, on_device(): lax.ppermute(part.astype(jnp.float16), 'off', back).astype(jnp.float32)  4.62 us
    ppermute x1, waiting for transfers between devices, deep_layers(): other = lax.ppermute(edges[0], 'depth', [(0, 1), (1, 0)])  1.71 us
    ppermute x1, starting transfers between devices, deep_layers(): other = lax.ppermute(edges[0], 'depth', [(0, 1), (1, 0)])  1.36 us
    pallas_call x3, Pallas kernels, source_of(): pl.pallas_call(functools.partial(source_kernel, half_span, step, groups),...  1.34 us
    ppermute x3, waiting for transfers between devices, on_device(): lax.ppermute(part.astype(jnp.float16), 'off', back).astype(jnp.float32)  1.17 us
    pallas_call x1, Pallas kernels, moved(): pl.pallas_call(move_kernel, out_shape=[space(x.shape, x.dtype) for x, spa...  0.94 us
    pallas_call x1, Pallas kernels, on_device(): pl.pallas_call(functools.partial(step_kernel, half_span), out_shape=pltpu...  0.83 us
  transfers between devices with their start and end apart: 7, of which 4 were waited for; matrix products, arithmetic and copies ran while one was open for 0% of the time, Pallas kernels for 16%

profile of v6, /device:TPU:0, one launch (start us, length us, event | category | flops | bytes accessed | tf_op | source)
XLA Modules:
  0.0 19.8 jit_solution(17399210668634109443)
XLA Ops:
  0.0 3.0 %collective-permute-start = (bf16[8,16,256]{2,1,0:T(8,128)(2,1)}, bf16[8,16,256]{2,1,0:T(8,128)(2,1)S(1)}, u32[]{:S(2)}, u32[]{:S(2)}) collective-permute-start(bf16[8,16,256]{2,1,0:T(8,128)(2,1)} %bitcast.7), channel_id=1, source_target_pairs={{0,4},{4,8},{8,12},{12,0},{1,5},{5,9},{9,13},{13,1},{2,6},{6,10},{... | collective-permute-start | bytes 196616 | tf_op jit(solution)/shard_map/ppermute | solution.py:195
  3.0 2.1 %collective-permute-start.2 = (bf16[8,16,256]{2,1,0:T(8,128)(2,1)}, bf16[8,16,256]{2,1,0:T(8,128)(2,1)S(1)}, u32[]{:S(2)}, u32[]{:S(2)}) collective-permute-start(bf16[8,16,256]{2,1,0:T(8,128)(2,1)} %bitcast.8), channel_id=1, source_target_pairs={{0,12},{4,0},{8,4},{12,8},{1,13},{5,1},{9,5},{13,9},{2,14},{6,2},{... | collective-permute-start | bytes 196616 | tf_op jit(solution)/shard_map/ppermute | solution.py:195
  5.1 1.0 %collective-permute-start.5 = (bf16[8,16,256]{2,1,0:T(8,128)(2,1)}, bf16[8,16,256]{2,1,0:T(8,128)(2,1)S(1)}, u32[]{:S(2)}, u32[]{:S(2)}) collective-permute-start(bf16[8,16,256]{2,1,0:T(8,128)(2,1)} %bitcast.9), channel_id=1, source_target_pairs={{0,8},{4,12},{8,0},{12,4},{1,9},{5,13},{9,1},{13,5},{2,10},{6,14},... | collective-permute-start | bytes 196616 | tf_op jit(solution)/shard_map/ppermute | solution.py:195
  6.1 0.9 %shard_map.64 = (f32[8,16,256]{2,1,0:T(8,128)S(1)}, s32[16]{0:T(128)S(4)}, bf16[8,16,256]{2,1,0:T(8,128)(2,1)S(1)}) custom-call(f32[8,16,256]{2,1,0:T(8,128)} %bitcast.6, s32[16]{0:T(128)} %refs_1_.1, bf16[8,16,256]{2,1,0:T(8,128)(2,1)} %bitcast.10), custom_call_target="tpu_custom_call" | custom-call | tf_op jit(solution)/shard_map/pallas_call | solution.py:70
  7.0 0.6 %collective-permute-done.background_ref = bf16[8,16,256]{2,1,0:T(8,128)(2,1)S(1)} collective-permute-done((bf16[8,16,256]{2,1,0:T(8,128)(2,1)}, bf16[8,16,256]{2,1,0:T(8,128)(2,1)S(1)}, u32[]{:S(2)}, u32[]{:S(2)}) %collective-permute-start) | collective-permute-done | bytes 65568 | tf_op jit(solution)/shard_map/ppermute | solution.py:195
  7.7 0.0 copy-done
  7.7 0.5 %shard_map.66 = (f32[12,16,256]{2,1,0:T(8,128)S(1)}, f32[8,4,256]{2,1,0:T(4,128)S(1)}) custom-call(s32[16]{0:T(128)S(4)} %get-tuple-element.10.offset_ref, bf16[16,32,16,256]{3,2,1,0:T(8,128)(2,1)S(1)} %copy-done, bf16[8,16,256]{2,1,0:T(8,128)(2,1)S(1)} %collective-permute-done.background_ref, f32[8,16,256]{2,1,0:T(8,128)S(1)} %get-tuple-element.12.now_ref.earlier_ref, ...), custom_call_target="tpu_custom_call" | custom-call | flops 1000 | bytes 1000 | tf_op jit(solution)/shard_map/pallas_call | solution.py:114
  8.1 0.1 collective-permute-done.2.background_ref
  8.2 0.4 %shard_map.68.earlier_ref = f32[12,16,256]{2,1,0:T(8,128)S(1)} custom-call(s32[16]{0:T(128)S(4)} %get-tuple-element.10.offset_ref, bf16[16,32,16,256]{3,2,1,0:T(8,128)(2,1)S(1)} %copy-done, bf16[8,16,256]{2,1,0:T(8,128)(2,1)S(1)} %collective-permute-done.2.background_ref, f32[8,16,256]{2,1,0:T(8,128)S(1)} %get-tuple-element.12.now_ref.earlier_ref, ...), custom_call_target="tpu_custom_call" | custom-call | flops 1000 | bytes 1000 | tf_op jit(solution)/shard_map/pallas_call | solution.py:114
  8.7 3.0 %collective-permute-start.3 = (f16[12,16,256]{2,1,0:T(8,128)(2,1)S(1)}, f16[12,16,256]{2,1,0:T(8,128)(2,1)S(1)}, u32[]{:S(2)}, u32[]{:S(2)}) collective-permute-start(f16[12,16,256]{2,1,0:T(8,128)(2,1)S(1)} %convert_element_type.22), channel_id=1, source_target_pairs={{0,4},{4,8},{8,12},{12,0},{1,5},{5,9},{9,13},{13,1},{2,6},{6,10},{... | collective-permute-start | bytes 294920 | tf_op jit(solution)/shard_map/ppermute | solution.py:217
  11.7 0.9 %collective-permute-start.4 = (f16[12,16,256]{2,1,0:T(8,128)(2,1)S(1)}, f16[12,16,256]{2,1,0:T(8,128)(2,1)S(1)}, u32[]{:S(2)}, u32[]{:S(2)}) collective-permute-start(f16[12,16,256]{2,1,0:T(8,128)(2,1)S(1)} %convert_element_type.24), channel_id=1, source_target_pairs={{0,12},{4,0},{8,4},{12,8},{1,13},{5,1},{9,5},{13,9},{2,14},{6,2},{... | collective-permute-start | bytes 294920 | tf_op jit(solution)/shard_map/ppermute | solution.py:217
  12.6 0.0 collective-permute-done.5.background_ref
  12.6 0.4 %shard_map.69 = f32[8,16,256]{2,1,0:T(8,128)S(1)} custom-call(s32[16]{0:T(128)S(4)} %get-tuple-element.10.offset_ref, bf16[16,32,16,256]{3,2,1,0:T(8,128)(2,1)S(1)} %copy-done, bf16[8,16,256]{2,1,0:T(8,128)(2,1)S(1)} %collective-permute-done.5.background_ref, f32[8,16,256]{2,1,0:T(8,128)S(1)} %get-tuple-element.12.now_ref.earlier_ref, ...), custom_call_target="tpu_custom_call" | custom-call | flops 1000 | bytes 1000 | tf_op jit(solution)/shard_map/pallas_call | solution.py:114
  13.1 0.7 %collective-permute-start.6 = (f16[8,16,256]{2,1,0:T(8,128)(2,1)S(1)}, f16[8,16,256]{2,1,0:T(8,128)(2,1)S(1)}, u32[]{:S(2)}, u32[]{:S(2)}) collective-permute-start(f16[8,16,256]{2,1,0:T(8,128)(2,1)S(1)} %convert_element_type.26), channel_id=1, source_target_pairs={{0,8},{4,12},{8,0},{12,4},{1,9},{5,13},{9,1},{13,5},{2,10},{6,14},... | collective-permute-start | bytes 196616 | tf_op jit(solution)/shard_map/ppermute | solution.py:217
  13.8 1.4 %collective-permute-start.1 = (f32[8,4,256]{2,1,0:T(4,128)S(1)}, f32[8,4,256]{2,1,0:T(4,128)S(1)}, u32[]{:S(2)}, u32[]{:S(2)}) collective-permute-start(f32[8,4,256]{2,1,0:T(4,128)S(1)} %get-tuple-element.13), channel_id=1, source_target_pairs={{0,2},{2,0},{1,3},{3,1},{4,6},{6,4},{5,7},{7,5},{8,10},{10,8},{9,1... | collective-permute-start | bytes 98312 | tf_op jit(solution)/shard_map/ppermute | solution.py:180
  15.2 0.0 copy-done.1
  15.2 0.0 copy-done.2
  15.2 0.8 %shard_map.65.base_ref = f32[8,16,256]{2,1,0:T(8,128)S(1)} custom-call(s32[16]{0:T(128)S(4)} %get-tuple-element.10.offset_ref, bf16[16,32,16,256]{3,2,1,0:T(8,128)(2,1)S(1)} %copy-done, bf16[8,16,256]{2,1,0:T(8,128)(2,1)S(1)} %get-tuple-element.11.background_ref, f32[8,16,256]{2,1,0:T(8,128)S(1)} %get-tuple-element.12.now_ref.earlier_ref, ...), custom_call_target="tpu_custom_call" | custom-call | flops 1000 | bytes 1000 | tf_op jit(solution)/shard_map/pallas_call | solution.py:220
  16.0 1.7 %collective-permute-done.1.above_ref.below_ref = f32[8,4,256]{2,1,0:T(4,128)S(1)} collective-permute-done((f32[8,4,256]{2,1,0:T(4,128)S(1)}, f32[8,4,256]{2,1,0:T(4,128)S(1)}, u32[]{:S(2)}, u32[]{:S(2)}) %collective-permute-start.1) | collective-permute-done | bytes 32800 | tf_op jit(solution)/shard_map/ppermute | solution.py:180
  17.7 0.1 shard_map.67
  17.8 0.0 collective-permute-done.3
  17.9 0.0 collective-permute-done.4
  17.9 1.2 %collective-permute-done.6 = f16[8,16,256]{2,1,0:T(8,128)(2,1)S(1)} collective-permute-done((f16[8,16,256]{2,1,0:T(8,128)(2,1)S(1)}, f16[8,16,256]{2,1,0:T(8,128)(2,1)S(1)}, u32[]{:S(2)}, u32[]{:S(2)}) %collective-permute-start.6) | collective-permute-done | bytes 65568 | tf_op jit(solution)/shard_map/ppermute | solution.py:217
  19.1 0.7 %fusion.7 = f32[1,8,16,256]{3,2,1,0:T(8,128)} fusion(f32[8,16,256]{2,1,0:T(8,128)S(1)} %shard_map.67, f32[8,16,256]{2,1,0:T(8,128)S(1)} %copy-done.1, f32[4,16,256]{2,1,0:T(8,128)S(1)} %slice.50, f32[4,16,256]{2,1,0:T(8,128)S(1)} %slice.51, f32[12,16,256]{2,1,0:T(8,128)S(1)} %convert_element_type.25, f32[12,16,256]{2,1,0:T(8,128)S(1)} %convert_element_type.23, ...), kind=kLoop, calls=%fused_computation.21 | loop fusion | flops 851968 | bytes 851968 | tf_op jit(solution)/shard_map/broadcast_in_dim | solution.py:248
  (10 shorter events, 0.1 us)
Async XLA Ops:
  0.0 7.7 %copy-start = (bf16[16,32,16,256]{3,2,1,0:T(8,128)(2,1)S(1)}, bf16[16,32,16,256]{3,2,1,0:T(8,128)(2,1)}, u32[]{:S(2)}) copy-start(bf16[16,32,16,256]{3,2,1,0:T(8,128)(2,1)} %image_ref.7) | copy-start | bytes 12582916
  0.0 7.7 %collective-permute-start = (bf16[8,16,256]{2,1,0:T(8,128)(2,1)}, bf16[8,16,256]{2,1,0:T(8,128)(2,1)S(1)}, u32[]{:S(2)}, u32[]{:S(2)}) collective-permute-start(bf16[8,16,256]{2,1,0:T(8,128)(2,1)} %bitcast.7), channel_id=1, source_target_pairs={{0,4},{4,8},{8,12},{12,0},{1,5},{5,9},{9,13},{13,1},{2,6},{6,10},{... | collective-permute-start | bytes 196616 | tf_op jit(solution)/shard_map/ppermute | solution.py:195
  3.0 5.2 %collective-permute-start.2 = (bf16[8,16,256]{2,1,0:T(8,128)(2,1)}, bf16[8,16,256]{2,1,0:T(8,128)(2,1)S(1)}, u32[]{:S(2)}, u32[]{:S(2)}) collective-permute-start(bf16[8,16,256]{2,1,0:T(8,128)(2,1)} %bitcast.8), channel_id=1, source_target_pairs={{0,12},{4,0},{8,4},{12,8},{1,13},{5,1},{9,5},{13,9},{2,14},{6,2},{... | collective-permute-start | bytes 196616 | tf_op jit(solution)/shard_map/ppermute | solution.py:195
  5.1 7.5 %collective-permute-start.5 = (bf16[8,16,256]{2,1,0:T(8,128)(2,1)}, bf16[8,16,256]{2,1,0:T(8,128)(2,1)S(1)}, u32[]{:S(2)}, u32[]{:S(2)}) collective-permute-start(bf16[8,16,256]{2,1,0:T(8,128)(2,1)} %bitcast.9), channel_id=1, source_target_pairs={{0,8},{4,12},{8,0},{12,4},{1,9},{5,13},{9,1},{13,5},{2,10},{6,14},... | collective-permute-start | bytes 196616 | tf_op jit(solution)/shard_map/ppermute | solution.py:195
  8.2 7.0 %copy-start.1 = (f32[8,16,256]{2,1,0:T(8,128)S(1)}, f32[8,16,256]{2,1,0:T(8,128)}, u32[]{:S(2)}) copy-start(f32[8,16,256]{2,1,0:T(8,128)} %courant_ref.3) | copy-start | bytes 393220
  8.2 7.0 %copy-start.2 = (f32[1,8,16,256]{3,2,1,0:T(8,128)S(1)}, f32[1,8,16,256]{3,2,1,0:T(8,128)}, u32[]{:S(2)}) copy-start(f32[1,8,16,256]{3,2,1,0:T(8,128)} %param.10) | copy-start | bytes 393220
  8.7 9.1 %collective-permute-start.3 = (f16[12,16,256]{2,1,0:T(8,128)(2,1)S(1)}, f16[12,16,256]{2,1,0:T(8,128)(2,1)S(1)}, u32[]{:S(2)}, u32[]{:S(2)}) collective-permute-start(f16[12,16,256]{2,1,0:T(8,128)(2,1)S(1)} %convert_element_type.22), channel_id=1, source_target_pairs={{0,4},{4,8},{8,12},{12,0},{1,5},{5,9},{9,13},{13,1},{2,6},{6,10},{... | collective-permute-start | bytes 294920 | tf_op jit(solution)/shard_map/ppermute | solution.py:217
  11.7 6.1 %collective-permute-start.4 = (f16[12,16,256]{2,1,0:T(8,128)(2,1)S(1)}, f16[12,16,256]{2,1,0:T(8,128)(2,1)S(1)}, u32[]{:S(2)}, u32[]{:S(2)}) collective-permute-start(f16[12,16,256]{2,1,0:T(8,128)(2,1)S(1)} %convert_element_type.24), channel_id=1, source_target_pairs={{0,12},{4,0},{8,4},{12,8},{1,13},{5,1},{9,5},{13,9},{2,14},{6,2},{... | collective-permute-start | bytes 294920 | tf_op jit(solution)/shard_map/ppermute | solution.py:217
  13.1 6.0 %collective-permute-start.6 = (f16[8,16,256]{2,1,0:T(8,128)(2,1)S(1)}, f16[8,16,256]{2,1,0:T(8,128)(2,1)S(1)}, u32[]{:S(2)}, u32[]{:S(2)}) collective-permute-start(f16[8,16,256]{2,1,0:T(8,128)(2,1)S(1)} %convert_element_type.26), channel_id=1, source_target_pairs={{0,8},{4,12},{8,0},{12,4},{1,9},{5,13},{9,1},{13,5},{2,10},{6,14},... | collective-permute-start | bytes 196616 | tf_op jit(solution)/shard_map/ppermute | solution.py:217
  13.8 3.9 %collective-permute-start.1 = (f32[8,4,256]{2,1,0:T(4,128)S(1)}, f32[8,4,256]{2,1,0:T(4,128)S(1)}, u32[]{:S(2)}, u32[]{:S(2)}) collective-permute-start(f32[8,4,256]{2,1,0:T(4,128)S(1)} %get-tuple-element.13), channel_id=1, source_target_pairs={{0,2},{2,0},{1,3},{3,1},{4,6},{6,4},{5,7},{7,5},{8,10},{10,8},{9,1... | collective-permute-start | bytes 98312 | tf_op jit(solution)/shard_map/ppermute | solution.py:180

commit v7 on v5

--- a/solution.py
+++ b/solution.py
@@ -189,12 +189,11 @@
     groups = lax.axis_size("off")
     own_slab, prev = background[0], wave_prev[0]
 
-    slabs = {}
+    def sent(cells, step):
+        return lax.ppermute(cells, "off", [(i, (i + step) % groups) for i in range(groups)])
+
     order = sorted(range(1, groups), key=lambda step: min(step, groups - step))
-    for step in order:
-        slabs[step] = lax.ppermute(
-            own_slab, "off", [(i, (i + step) % groups) for i in range(groups)]
-        )
+    slabs = {step: sent(own_slab, step) for step in order[:2]}
     held = pltpu.with_memory_space_constraint(image, pltpu.VMEM)
     now, cells, own_slab = moved(
         image,
@@ -202,6 +201,7 @@
         (offset_of, pltpu.SMEM),
         (own_slab, pltpu.VMEM),
     )
+    slabs.update({step: sent(own_slab, step) for step in order[2:]})
     rows, depth, width = now.shape
 
     returned = {}

time: 19.9 us -> 20 us (level)
  starting transfers between devices: 12 us -> 12.4 us
  waiting for transfers between devices: 3.61 us -> 3.27 us
    ppermute x1, starting transfers between devices: 1.36 us -> 1.63 us  [deep_layers(): other = lax.ppermute(edges[0], 'depth', [(0, 1), (1, 0)])]
    ppermute x1, waiting for transfers between devices: 1.71 us -> 1.44 us  [deep_layers(): other = lax.ppermute(edges[0], 'depth', [(0, 1), (1, 0)])]
where the time goes in v7:
time: 20 us; the launch traced here: 19.8 us
  starting transfers between devices  12.4 us (62%)
  waiting for transfers between devices  3.27 us (16%)
  Pallas kernels  3.19 us (16%)
  other arithmetic  0.8 us (4%)
    ppermute x3, starting transfers between devices, sent(): lax.ppermute(cells, 'off', [(i, (i + step) % groups) for i in range(group...  6.13 us
    ppermute x3, starting transfers between devices, on_device(): lax.ppermute(part.astype(jnp.float16), 'off', back).astype(jnp.float32)  4.66 us
    ppermute x1, starting transfers between devices, deep_layers(): other = lax.ppermute(edges[0], 'depth', [(0, 1), (1, 0)])  1.63 us
    ppermute x1, waiting for transfers between devices, deep_layers(): other = lax.ppermute(edges[0], 'depth', [(0, 1), (1, 0)])  1.44 us
    pallas_call x3, Pallas kernels, source_of(): pl.pallas_call(functools.partial(source_kernel, half_span, step, groups),...  1.34 us
    ppermute x3, waiting for transfers between devices, on_device(): lax.ppermute(part.astype(jnp.float16), 'off', back).astype(jnp.float32)  1.16 us
    pallas_call x1, Pallas kernels, moved(): pl.pallas_call(move_kernel, out_shape=[space(x.shape, x.dtype) for x, spa...  0.94 us
    pallas_call x1, Pallas kernels, on_device(): pl.pallas_call(functools.partial(step_kernel, half_span), out_shape=pltpu...  0.83 us
  transfers between devices with their start and end apart: 7, of which 4 were waited for; matrix products, arithmetic and copies ran while one was open for 0% of the time, Pallas kernels for 16%

profile of v7, /device:TPU:0, one launch (start us, length us, event | category | flops | bytes accessed | tf_op | source)
XLA Modules:
  0.0 19.8 jit_solution(12909113931364907390)
XLA Ops:
  0.0 3.0 %collective-permute-start = (bf16[8,16,256]{2,1,0:T(8,128)(2,1)}, bf16[8,16,256]{2,1,0:T(8,128)(2,1)S(1)}, u32[]{:S(2)}, u32[]{:S(2)}) collective-permute-start(bf16[8,16,256]{2,1,0:T(8,128)(2,1)} %bitcast.7), channel_id=1, source_target_pairs={{0,4},{4,8},{8,12},{12,0},{1,5},{5,9},{9,13},{13,1},{2,6},{6,10},{... | collective-permute-start | bytes 196616 | tf_op jit(solution)/shard_map/ppermute | solution.py:193
  3.0 2.1 %collective-permute-start.2 = (bf16[8,16,256]{2,1,0:T(8,128)(2,1)}, bf16[8,16,256]{2,1,0:T(8,128)(2,1)S(1)}, u32[]{:S(2)}, u32[]{:S(2)}) collective-permute-start(bf16[8,16,256]{2,1,0:T(8,128)(2,1)} %bitcast.8), channel_id=1, source_target_pairs={{0,12},{4,0},{8,4},{12,8},{1,13},{5,1},{9,5},{13,9},{2,14},{6,2},{... | collective-permute-start | bytes 196616 | tf_op jit(solution)/shard_map/ppermute | solution.py:193
  5.1 0.9 %shard_map.64 = (f32[8,16,256]{2,1,0:T(8,128)S(1)}, s32[16]{0:T(128)S(4)}, bf16[8,16,256]{2,1,0:T(8,128)(2,1)S(1)}) custom-call(f32[8,16,256]{2,1,0:T(8,128)} %bitcast.6, s32[16]{0:T(128)} %refs_1_.1, bf16[8,16,256]{2,1,0:T(8,128)(2,1)} %bitcast.9), custom_call_target="tpu_custom_call" | custom-call | tf_op jit(solution)/shard_map/pallas_call | solution.py:70
  6.1 1.0 %collective-permute-start.4 = (bf16[8,16,256]{2,1,0:T(8,128)(2,1)S(1)}, bf16[8,16,256]{2,1,0:T(8,128)(2,1)S(1)}, u32[]{:S(2)}, u32[]{:S(2)}) collective-permute-start(bf16[8,16,256]{2,1,0:T(8,128)(2,1)S(1)} %get-tuple-element.11.background_ref), channel_id=1, source_target_pairs={{0,8},{4,12},{8,0},{12,4},{1,9},{5,13},{9,1},{13,5},{2,10},{6,14},... | collective-permute-start | bytes 196616 | tf_op jit(solution)/shard_map/ppermute | solution.py:193
  7.1 0.6 %collective-permute-done.background_ref = bf16[8,16,256]{2,1,0:T(8,128)(2,1)S(1)} collective-permute-done((bf16[8,16,256]{2,1,0:T(8,128)(2,1)}, bf16[8,16,256]{2,1,0:T(8,128)(2,1)S(1)}, u32[]{:S(2)}, u32[]{:S(2)}) %collective-permute-start) | collective-permute-done | bytes 65568 | tf_op jit(solution)/shard_map/ppermute | solution.py:193
  7.7 0.0 copy-done
  7.7 0.5 %shard_map.66 = (f32[12,16,256]{2,1,0:T(8,128)S(1)}, f32[8,4,256]{2,1,0:T(4,128)S(1)}) custom-call(s32[16]{0:T(128)S(4)} %get-tuple-element.10.offset_ref, bf16[16,32,16,256]{3,2,1,0:T(8,128)(2,1)S(1)} %copy-done, bf16[8,16,256]{2,1,0:T(8,128)(2,1)S(1)} %collective-permute-done.background_ref, f32[8,16,256]{2,1,0:T(8,128)S(1)} %get-tuple-element.12.now_ref.earlier_ref, ...), custom_call_target="tpu_custom_call" | custom-call | flops 1000 | bytes 1000 | tf_op jit(solution)/shard_map/pallas_call | solution.py:114
  8.1 0.1 collective-permute-done.2.background_ref
  8.2 0.4 %shard_map.68.earlier_ref = f32[12,16,256]{2,1,0:T(8,128)S(1)} custom-call(s32[16]{0:T(128)S(4)} %get-tuple-element.10.offset_ref, bf16[16,32,16,256]{3,2,1,0:T(8,128)(2,1)S(1)} %copy-done, bf16[8,16,256]{2,1,0:T(8,128)(2,1)S(1)} %collective-permute-done.2.background_ref, f32[8,16,256]{2,1,0:T(8,128)S(1)} %get-tuple-element.12.now_ref.earlier_ref, ...), custom_call_target="tpu_custom_call" | custom-call | flops 1000 | bytes 1000 | tf_op jit(solution)/shard_map/pallas_call | solution.py:114
  8.7 2.1 %collective-permute-start.3 = (f16[12,16,256]{2,1,0:T(8,128)(2,1)S(1)}, f16[12,16,256]{2,1,0:T(8,128)(2,1)S(1)}, u32[]{:S(2)}, u32[]{:S(2)}) collective-permute-start(f16[12,16,256]{2,1,0:T(8,128)(2,1)S(1)} %convert_element_type.18), channel_id=1, source_target_pairs={{0,4},{4,8},{8,12},{12,0},{1,5},{5,9},{9,13},{13,1},{2,6},{6,10},{... | collective-permute-start | bytes 294920 | tf_op jit(solution)/shard_map/ppermute | solution.py:217
  10.8 1.9 %collective-permute-start.6 = (f16[12,16,256]{2,1,0:T(8,128)(2,1)S(1)}, f16[12,16,256]{2,1,0:T(8,128)(2,1)S(1)}, u32[]{:S(2)}, u32[]{:S(2)}) collective-permute-start(f16[12,16,256]{2,1,0:T(8,128)(2,1)S(1)} %convert_element_type.22), channel_id=1, source_target_pairs={{0,12},{4,0},{8,4},{12,8},{1,13},{5,1},{9,5},{13,9},{2,14},{6,2},{... | collective-permute-start | bytes 294920 | tf_op jit(solution)/shard_map/ppermute | solution.py:217
  12.7 0.0 collective-permute-done.4.background_ref
  12.7 0.4 %shard_map.69 = f32[8,16,256]{2,1,0:T(8,128)S(1)} custom-call(s32[16]{0:T(128)S(4)} %get-tuple-element.10.offset_ref, bf16[16,32,16,256]{3,2,1,0:T(8,128)(2,1)S(1)} %copy-done, bf16[8,16,256]{2,1,0:T(8,128)(2,1)S(1)} %collective-permute-done.4.background_ref, f32[8,16,256]{2,1,0:T(8,128)S(1)} %get-tuple-element.12.now_ref.earlier_ref, ...), custom_call_target="tpu_custom_call" | custom-call | flops 1000 | bytes 1000 | tf_op jit(solution)/shard_map/pallas_call | solution.py:114
  13.2 0.6 %collective-permute-start.5 = (f16[8,16,256]{2,1,0:T(8,128)(2,1)S(1)}, f16[8,16,256]{2,1,0:T(8,128)(2,1)S(1)}, u32[]{:S(2)}, u32[]{:S(2)}) collective-permute-start(f16[8,16,256]{2,1,0:T(8,128)(2,1)S(1)} %convert_element_type.20), channel_id=1, source_target_pairs={{0,8},{4,12},{8,0},{12,4},{1,9},{5,13},{9,1},{13,5},{2,10},{6,14},... | collective-permute-start | bytes 196616 | tf_op jit(solution)/shard_map/ppermute | solution.py:217
  13.8 1.6 %collective-permute-start.1 = (f32[8,4,256]{2,1,0:T(4,128)S(1)}, f32[8,4,256]{2,1,0:T(4,128)S(1)}, u32[]{:S(2)}, u32[]{:S(2)}) collective-permute-start(f32[8,4,256]{2,1,0:T(4,128)S(1)} %get-tuple-element.13), channel_id=1, source_target_pairs={{0,2},{2,0},{1,3},{3,1},{4,6},{6,4},{5,7},{7,5},{8,10},{10,8},{9,1... | collective-permute-start | bytes 98312 | tf_op jit(solution)/shard_map/ppermute | solution.py:180
  15.5 0.0 copy-done.1
  15.5 0.0 copy-done.2
  15.5 0.8 %shard_map.65.base_ref = f32[8,16,256]{2,1,0:T(8,128)S(1)} custom-call(s32[16]{0:T(128)S(4)} %get-tuple-element.10.offset_ref, bf16[16,32,16,256]{3,2,1,0:T(8,128)(2,1)S(1)} %copy-done, bf16[8,16,256]{2,1,0:T(8,128)(2,1)S(1)} %get-tuple-element.11.background_ref, f32[8,16,256]{2,1,0:T(8,128)S(1)} %get-tuple-element.12.now_ref.earlier_ref, ...), custom_call_target="tpu_custom_call" | custom-call | flops 1000 | bytes 1000 | tf_op jit(solution)/shard_map/pallas_call | solution.py:220
  16.3 1.4 %collective-permute-done.1.above_ref.below_ref = f32[8,4,256]{2,1,0:T(4,128)S(1)} collective-permute-done((f32[8,4,256]{2,1,0:T(4,128)S(1)}, f32[8,4,256]{2,1,0:T(4,128)S(1)}, u32[]{:S(2)}, u32[]{:S(2)}) %collective-permute-start.1) | collective-permute-done | bytes 32800 | tf_op jit(solution)/shard_map/ppermute | solution.py:180
  17.8 0.1 shard_map.67
  17.8 0.0 collective-permute-done.3
  17.9 0.0 collective-permute-done.6
  17.9 1.2 %collective-permute-done.5 = f16[8,16,256]{2,1,0:T(8,128)(2,1)S(1)} collective-permute-done((f16[8,16,256]{2,1,0:T(8,128)(2,1)S(1)}, f16[8,16,256]{2,1,0:T(8,128)(2,1)S(1)}, u32[]{:S(2)}, u32[]{:S(2)}) %collective-permute-start.5) | collective-permute-done | bytes 65568 | tf_op jit(solution)/shard_map/ppermute | solution.py:217
  19.1 0.7 %fusion.9 = f32[1,8,16,256]{3,2,1,0:T(8,128)} fusion(f32[8,16,256]{2,1,0:T(8,128)S(1)} %shard_map.67, f32[8,16,256]{2,1,0:T(8,128)S(1)} %copy-done.1, f32[4,16,256]{2,1,0:T(8,128)S(1)} %slice.58, f32[4,16,256]{2,1,0:T(8,128)S(1)} %slice.59, f32[12,16,256]{2,1,0:T(8,128)S(1)} %convert_element_type.23, f32[12,16,256]{2,1,0:T(8,128)S(1)} %convert_element_type.19, ...), kind=kLoop, calls=%fused_computation.17 | loop fusion | flops 589824 | bytes 851968 | tf_op jit(solution)/shard_map/broadcast_in_dim | solution.py:247
  (10 shorter events, 0.1 us)
Async XLA Ops:
  0.0 7.7 %copy-start = (bf16[16,32,16,256]{3,2,1,0:T(8,128)(2,1)S(1)}, bf16[16,32,16,256]{3,2,1,0:T(8,128)(2,1)}, u32[]{:S(2)}) copy-start(bf16[16,32,16,256]{3,2,1,0:T(8,128)(2,1)} %image_ref.7) | copy-start | bytes 12582916
  0.0 7.7 %collective-permute-start = (bf16[8,16,256]{2,1,0:T(8,128)(2,1)}, bf16[8,16,256]{2,1,0:T(8,128)(2,1)S(1)}, u32[]{:S(2)}, u32[]{:S(2)}) collective-permute-start(bf16[8,16,256]{2,1,0:T(8,128)(2,1)} %bitcast.7), channel_id=1, source_target_pairs={{0,4},{4,8},{8,12},{12,0},{1,5},{5,9},{9,13},{13,1},{2,6},{6,10},{... | collective-permute-start | bytes 196616 | tf_op jit(solution)/shard_map/ppermute | solution.py:193
  3.0 5.2 %collective-permute-start.2 = (bf16[8,16,256]{2,1,0:T(8,128)(2,1)}, bf16[8,16,256]{2,1,0:T(8,128)(2,1)S(1)}, u32[]{:S(2)}, u32[]{:S(2)}) collective-permute-start(bf16[8,16,256]{2,1,0:T(8,128)(2,1)} %bitcast.8), channel_id=1, source_target_pairs={{0,12},{4,0},{8,4},{12,8},{1,13},{5,1},{9,5},{13,9},{2,14},{6,2},{... | collective-permute-start | bytes 196616 | tf_op jit(solution)/shard_map/ppermute | solution.py:193
  6.1 6.7 %collective-permute-start.4 = (bf16[8,16,256]{2,1,0:T(8,128)(2,1)S(1)}, bf16[8,16,256]{2,1,0:T(8,128)(2,1)S(1)}, u32[]{:S(2)}, u32[]{:S(2)}) collective-permute-start(bf16[8,16,256]{2,1,0:T(8,128)(2,1)S(1)} %get-tuple-element.11.background_ref), channel_id=1, source_target_pairs={{0,8},{4,12},{8,0},{12,4},{1,9},{5,13},{9,1},{13,5},{2,10},{6,14},... | collective-permute-start | bytes 196616 | tf_op jit(solution)/shard_map/ppermute | solution.py:193
  8.2 7.3 %copy-start.1 = (f32[8,16,256]{2,1,0:T(8,128)S(1)}, f32[8,16,256]{2,1,0:T(8,128)}, u32[]{:S(2)}) copy-start(f32[8,16,256]{2,1,0:T(8,128)} %courant_ref.3) | copy-start | bytes 393220
  8.2 7.3 %copy-start.2 = (f32[1,8,16,256]{3,2,1,0:T(8,128)S(1)}, f32[1,8,16,256]{3,2,1,0:T(8,128)}, u32[]{:S(2)}) copy-start(f32[1,8,16,256]{3,2,1,0:T(8,128)} %param.10) | copy-start | bytes 393220
  8.7 9.2 %collective-permute-start.3 = (f16[12,16,256]{2,1,0:T(8,128)(2,1)S(1)}, f16[12,16,256]{2,1,0:T(8,128)(2,1)S(1)}, u32[]{:S(2)}, u32[]{:S(2)}) collective-permute-start(f16[12,16,256]{2,1,0:T(8,128)(2,1)S(1)} %convert_element_type.18), channel_id=1, source_target_pairs={{0,4},{4,8},{8,12},{12,0},{1,5},{5,9},{9,13},{13,1},{2,6},{6,10},{... | collective-permute-start | bytes 294920 | tf_op jit(solution)/shard_map/ppermute | solution.py:217
  10.8 7.1 %collective-permute-start.6 = (f16[12,16,256]{2,1,0:T(8,128)(2,1)S(1)}, f16[12,16,256]{2,1,0:T(8,128)(2,1)S(1)}, u32[]{:S(2)}, u32[]{:S(2)}) collective-permute-start(f16[12,16,256]{2,1,0:T(8,128)(2,1)S(1)} %convert_element_type.22), channel_id=1, source_target_pairs={{0,12},{4,0},{8,4},{12,8},{1,13},{5,1},{9,5},{13,9},{2,14},{6,2},{... | collective-permute-start | bytes 294920 | tf_op jit(solution)/shard_map/ppermute | solution.py:217
  13.2 5.9 %collective-permute-start.5 = (f16[8,16,256]{2,1,0:T(8,128)(2,1)S(1)}, f16[8,16,256]{2,1,0:T(8,128)(2,1)S(1)}, u32[]{:S(2)}, u32[]{:S(2)}) collective-permute-start(f16[8,16,256]{2,1,0:T(8,128)(2,1)S(1)} %convert_element_type.20), channel_id=1, source_target_pairs={{0,8},{4,12},{8,0},{12,4},{1,9},{5,13},{9,1},{13,5},{2,10},{6,14},... | collective-permute-start | bytes 196616 | tf_op jit(solution)/shard_map/ppermute | solution.py:217
  13.8 3.9 %collective-permute-start.1 = (f32[8,4,256]{2,1,0:T(4,128)S(1)}, f32[8,4,256]{2,1,0:T(4,128)S(1)}, u32[]{:S(2)}, u32[]{:S(2)}) collective-permute-start(f32[8,4,256]{2,1,0:T(4,128)S(1)} %get-tuple-element.13), channel_id=1, source_target_pairs={{0,2},{2,0},{1,3},{3,1},{4,6},{6,4},{5,7},{7,5},{8,10},{10,8},{9,1... | collective-permute-start | bytes 98312 | tf_op jit(solution)/shard_map/ppermute | solution.py:180
